TPU v7x, 32 devices: a whole 2x2x4 slice. The times are simulated.
32 devices in a mesh: dp: 4 (over y, x), expert: 8 (over z, core).
Axes of the slice: x: 2, y: 2, z: 4, core: 2. Of those that a mesh axis runs over, the one named last changes fastest.
Arguments:
- latent: bfloat16 [4096, 1024], P(('dp', 'expert')), may hold values from -6 to 6
- cotangent: bfloat16 [4096, 1024], P(('dp', 'expert')), may hold values from -0.59765625 to 0.59765625
- routes: int32 [4096, 1], P(('dp', 'expert')), may hold values from 0 to 7; in each aligned block of 128 rows (0 to 127, 128 to 255, ...) at most 32 rows name the same one
- gates: float32 [4096, 1], P(('dp', 'expert')), may hold values from 0.1 to 1
- w_in: bfloat16 [8, 1024, 2048], P('expert'), may hold values from -0.1875 to 0.1875
- w_out: bfloat16 [8, 1024, 1024], P('expert'), may hold values from -0.1875 to 0.1875
Outputs:
- output: bfloat16 [4096, 1024], P(('dp', 'expert'))
- grad_in: float32 [8, 1024, 2048], P('expert', 'dp')
- grad_out: float32 [8, 1024, 1024], P('expert', 'dp')
Inputs may be any that keep to these rules, and one draw needn't show every extreme that they name: In each aligned block of 128 tokens no expert is named by more than 32 routes, a bound that some block reaches.
All inputs are finite; a program needn't handle non-finite values.
Results may differ from a plain program's by a relative error of at most 0.018.
Values may be sent and summed in bfloat16 or wider, within the bound.
A program may use at most 64 MiB of HBM per device.

v0:
```python
import jax
import jax.numpy as jnp
from jax import lax
from jax.sharding import PartitionSpec as P


def on_device(latent, cotangent, routes, gates, w_in, w_out):
    n_experts = lax.axis_size("expert")
    n_replicas = lax.axis_size("dp")
    tok_count = latent.shape[0]
    top_count = routes.shape[1]
    width = latent.shape[1]
    hidden_units = w_out.shape[2]
    capacity = max(2, 2 * tok_count * top_count // n_experts)
    route_flat = routes.reshape(-1)
    gate_flat = gates.reshape(-1)
    onehot = (route_flat[:, None] == jnp.arange(n_experts, dtype=jnp.int32)[None, :]).astype(
        jnp.int32
    )
    before = jnp.cumsum(onehot, axis=0) - onehot
    slot = jnp.sum(before * onehot, axis=1)
    position = route_flat * capacity + slot
    placing = (
        jnp.arange(n_experts * capacity, dtype=jnp.int32)[:, None] == position[None, :]
    ).astype(jnp.bfloat16)
    x_rows = jnp.repeat(latent, top_count, axis=0)
    dy_rows = (
        gate_flat[:, None] * jnp.repeat(cotangent, top_count, axis=0).astype(jnp.float32)
    ).astype(jnp.bfloat16)
    send_x = (
        jnp.dot(placing, x_rows, preferred_element_type=jnp.float32)
        .astype(jnp.bfloat16)
        .reshape(n_experts, capacity, width)
    )
    send_dy = (
        jnp.dot(placing, dy_rows, preferred_element_type=jnp.float32)
        .astype(jnp.bfloat16)
        .reshape(n_experts, capacity, width)
    )
    got_x = lax.all_to_all(send_x, "expert", split_axis=0, concat_axis=0, tiled=True)
    got_dy = None
    x_buf = got_x.reshape(-1, width)
    acts = jnp.dot(x_buf, w_in[0], preferred_element_type=jnp.float32)
    gate = acts[:, :hidden_units]
    upper = acts[:, hidden_units:]
    sig = jax.nn.sigmoid(gate)
    swish = gate * sig
    hidden = (swish * upper).astype(jnp.bfloat16)
    y_buf = lax.dot_general(
        hidden, w_out[0], (((1,), (1,)), ((), ())), preferred_element_type=jnp.float32
    ).astype(jnp.bfloat16)
    back = lax.all_to_all(
        y_buf.reshape(n_experts, capacity, width), "expert", split_axis=0, concat_axis=0, tiled=True
    ).reshape(-1, width)
    y_rows = lax.dot_general(
        placing, back, (((0,), (0,)), ((), ())), preferred_element_type=jnp.float32
    )
    output = jnp.sum(
        (gate_flat[:, None] * y_rows).reshape(tok_count, top_count, width), axis=1
    ).astype(jnp.bfloat16)
    got_dy = lax.all_to_all(send_dy, "expert", split_axis=0, concat_axis=0, tiled=True)
    dy_buf = got_dy.reshape(-1, width)
    d_hidden = jnp.dot(dy_buf, w_out[0], preferred_element_type=jnp.float32)
    d_gate = d_hidden * upper * sig * (1.0 + gate * (1.0 - sig))
    d_upper = d_hidden * swish
    d_acts = jnp.concatenate([d_gate, d_upper], axis=1).astype(jnp.bfloat16)
    share = width // n_replicas
    columns = x_buf
    grad_in = lax.psum_scatter(
        lax.dot_general(
            columns, d_acts, (((0,), (0,)), ((), ())), preferred_element_type=jnp.float32
        ).astype(jnp.bfloat16),
        "dp",
        scatter_dimension=0,
        tiled=True,
    ).astype(jnp.float32)
    columns = dy_buf
    grad_out = lax.psum_scatter(
        lax.dot_general(
            columns, hidden, (((0,), (0,)), ((), ())), preferred_element_type=jnp.float32
        ).astype(jnp.bfloat16),
        "dp",
        scatter_dimension=0,
        tiled=True,
    ).astype(jnp.float32)
    return (
        output,
        grad_in.reshape(1, share, 2 * hidden_units),
        grad_out.reshape(1, share, hidden_units),
    )


def solution(mesh):
    in_specs = (
        P(("dp", "expert"), None),
        P(("dp", "expert"), None),
        P(("dp", "expert"), None),
        P(("dp", "expert"), None),
        P("expert", None, None),
        P("expert", None, None),
    )
    out_specs = (P(("dp", "expert"), None), P("expert", "dp", None), P("expert", "dp", None))
    return jax.shard_map(
        on_device, mesh=mesh, in_specs=in_specs, out_specs=out_specs, check_vma=False
    )
```

profile of v0, /device:TPU:9, one launch (start us, length us, event | category | flops | bytes accessed | tf_op | source)
XLA Modules:
  0.0 157.1 jit_solution(5826377989956109828)
XLA Ops:
  7.2 0.9 fusion.18
  8.1 0.2 reduce_window_sum.11
  8.3 0.8 select_reduce_fusion
  9.1 0.7 multiply_add_fusion
  9.8 2.0 %convolution_convert_fusion.3 = bf16[256,1024]{1,0:T(8,128)(2,1)} fusion(bf16[128,1024]{1,0:T(8,128)(2,1)} %param.6, s32[128]{0:T(128)S(1)} %multiply_add_fusion), kind=kOutput, calls=%fused_computation.10 | convolution fusion | flops 67403776 | bytes 786944 | tf_op jit(solution)/shard_map/dot_general | solution.py:31
  11.8 5.6 %all-to-all-start = ((bf16[8,32,1024]{2,1,0:T(8,128)(2,1)}), bf16[8,32,1024]{2,1,0:T(8,128)(2,1)S(1)}, u32[]{:S(2)}, u32[]{:S(2)}) async-start(bf16[8,32,1024]{2,1,0:T(8,128)(2,1)} %bitcast.2), calls=%async_computation | async-start | bytes 1048576 | tf_op jit(solution)/shard_map/all_to_all | solution.py:40
  17.4 1.2 convolution_convert_fusion.2
  18.6 10.6 %all-to-all-done = bf16[8,32,1024]{2,1,0:T(8,128)(2,1)S(1)} async-done(((bf16[8,32,1024]{2,1,0:T(8,128)(2,1)}), bf16[8,32,1024]{2,1,0:T(8,128)(2,1)S(1)}, u32[]{:S(2)}, u32[]{:S(2)}) %all-to-all-start) | async-done | bytes 524320 | tf_op jit(solution)/shard_map/all_to_all | solution.py:40
  29.2 7.0 %all-to-all-start.2 = ((bf16[8,32,1024]{2,1,0:T(8,128)(2,1)}), bf16[8,32,1024]{2,1,0:T(8,128)(2,1)S(1)}, u32[]{:S(2)}, u32[]{:S(2)}) async-start(bf16[8,32,1024]{2,1,0:T(8,128)(2,1)} %bitcast.8), calls=%async_computation.2 | async-start | bytes 1048576 | tf_op jit(solution)/shard_map/all_to_all | solution.py:61
  36.2 4.8 %fusion = f32[256,2048]{1,0:T(8,128)} fusion(bf16[256,1024]{1,0:T(8,128)(2,1)S(1)} %bitcast.35, bf16[1,1024,2048]{2,1,0:T(8,128)(2,1)} %param.10), kind=kOutput, calls=%fused_computation | convolution fusion | flops 1073741824 | bytes 6815744 | tf_op jit(solution)/shard_map/dot_general | solution.py:43
  41.0 7.0 %all-to-all-done.2 = bf16[8,32,1024]{2,1,0:T(8,128)(2,1)S(1)} async-done(((bf16[8,32,1024]{2,1,0:T(8,128)(2,1)}), bf16[8,32,1024]{2,1,0:T(8,128)(2,1)S(1)}, u32[]{:S(2)}, u32[]{:S(2)}) %all-to-all-start.2) | async-done | bytes 524320 | tf_op jit(solution)/shard_map/all_to_all | solution.py:61
  48.0 3.6 %multiply_convert_fusion.1 = (bf16[256,1024]{1,0:T(8,128)(2,1)}, bf16[256,1024]{1,0:T(8,128)(2,1)}, bf16[256,1024]{1,0:T(8,128)(2,1)S(1)}) fusion(f32[256,2048]{1,0:T(8,128)} %fusion, bf16[256,1024]{1,0:T(8,128)(2,1)S(1)} %bitcast.38, bf16[1,1024,1024]{2,1,0:T(8,128)(2,1)S(1)} %copy-done), kind=kOutput, calls=%fused_computation.18 | convolution fusion | flops 540803072 | bytes 6291456 | tf_op jit(solution)/shard_map/dot_general | solution.py:63
  51.6 0.8 copy-done.1
  52.4 2.1 %convolution_convert_fusion.1 = bf16[1024,1024]{1,0:T(8,128)(2,1)} fusion(bf16[256,1024]{1,0:T(8,128)(2,1)S(1)} %bitcast.39, bf16[256,1024]{1,0:T(8,128)(2,1)S(1)} %get-tuple-element.5), kind=kOutput, calls=%fused_computation.7 | convolution fusion | flops 537919488 | bytes 3145728 | tf_op jit(solution)/shard_map/dot_general | solution.py:79
  54.5 1.0 copy-done.3
  55.5 4.3 %convolution_convert_fusion = bf16[1024,2048]{1,0:T(8,128)(2,1)} fusion(bf16[256,1024]{1,0:T(8,128)(2,1)S(1)} %bitcast.36, bf16[256,1024]{1,0:T(8,128)(2,1)} %get-tuple-element.4, bf16[256,1024]{1,0:T(8,128)(2,1)S(1)} %copy-done.3), kind=kOutput, calls=%fused_computation.2 | convolution fusion | flops 1077936128 | bytes 5767168 | tf_op jit(solution)/shard_map/dot_general | solution.py:70
  59.8 1.0 copy-done.2
  60.8 0.7 fusion.6
  61.5 18.2 %all_to_all.15 = bf16[8,32,1024]{2,1,0:T(8,128)(2,1)S(1)} all-to-all(bf16[8,32,1024]{2,1,0:T(8,128)(2,1)S(1)} %bitcast.40), channel_id=1, replica_groups=mesh['dp'=4,'expert'=8] {'expert'}, dimensions={0} | all-to-all | bytes 1048576 | tf_op jit(solution)/shard_map/all_to_all | solution.py:52
  79.8 1.0 fusion.9
  80.8 10.7 %reduce-scatter.5.cloned.1.call-done = bf16[256,1024]{1,0:T(8,128)(2,1)} async-done(((bf16[1024,1024]{1,0:T(8,128)(2,1)}), bf16[256,1024]{1,0:T(8,128)(2,1)}) %reduce-scatter.5.cloned.1.call-update) | async-done | bytes 524304 | tf_op jit(solution)/shard_map/reduce_scatter | solution.py:78
  91.5 2.1 %bitcast_convert_fusion.1 = f32[1,256,1024]{2,1,0:T(8,128)} fusion(bf16[256,1024]{1,0:T(8,128)(2,1)} %reduce-scatter.5.cloned.1.call-done), kind=kLoop, calls=%fused_computation.22 | loop fusion | flops 262144 | bytes 1572864 | tf_op jit(solution)/shard_map/reshape | solution.py:89
  93.6 53.8 %reduce-scatter.3.cloned.1.call-done = bf16[256,2048]{1,0:T(8,128)(2,1)} async-done(((bf16[1024,2048]{1,0:T(8,128)(2,1)}), bf16[256,2048]{1,0:T(8,128)(2,1)}) %reduce-scatter.3.cloned.1.call-update) | async-done | bytes 1048592 | tf_op jit(solution)/shard_map/reduce_scatter | solution.py:69
  147.4 2.8 %bitcast_convert_fusion = f32[1,256,2048]{2,1,0:T(8,128)} fusion(bf16[256,2048]{1,0:T(8,128)(2,1)} %reduce-scatter.3.cloned.1.call-done), kind=kLoop, calls=%fused_computation.16 | loop fusion | flops 524288 | bytes 3145728 | tf_op jit(solution)/shard_map/reshape | solution.py:88
  (13 shorter events, 0.1 us)
Async XLA Ops:
  7.2 40.8 %copy-start = (bf16[1,1024,1024]{2,1,0:T(8,128)(2,1)S(1)}, bf16[1,1024,1024]{2,1,0:T(8,128)(2,1)}, u32[]{:S(2)}) copy-start(bf16[1,1024,1024]{2,1,0:T(8,128)(2,1)} %param.11) | copy-start | bytes 6291460
  7.2 10.3 %copy-start.5 = (f32[128,1]{0,1:T(1,128)S(1)}, f32[128,1]{0,1:T(1,128)}, u32[]{:S(2)}) copy-start(f32[128,1]{0,1:T(1,128)} %param.9) | copy-start | bytes 1540
  7.2 10.3 %copy-start.4 = (bf16[128,1024]{1,0:T(8,128)(2,1)S(1)}, bf16[128,1024]{1,0:T(8,128)(2,1)}, u32[]{:S(2)}) copy-start(bf16[128,1024]{1,0:T(8,128)(2,1)} %param.7) | copy-start | bytes 786436
  11.8 17.4 %all-to-all-start = ((bf16[8,32,1024]{2,1,0:T(8,128)(2,1)}), bf16[8,32,1024]{2,1,0:T(8,128)(2,1)S(1)}, u32[]{:S(2)}, u32[]{:S(2)}) async-start(bf16[8,32,1024]{2,1,0:T(8,128)(2,1)} %bitcast.2), calls=%async_computation | async-start | bytes 1048576 | tf_op jit(solution)/shard_map/all_to_all | solution.py:40
  29.2 18.8 %all-to-all-start.2 = ((bf16[8,32,1024]{2,1,0:T(8,128)(2,1)}), bf16[8,32,1024]{2,1,0:T(8,128)(2,1)S(1)}, u32[]{:S(2)}, u32[]{:S(2)}) async-start(bf16[8,32,1024]{2,1,0:T(8,128)(2,1)} %bitcast.8), calls=%async_computation.2 | async-start | bytes 1048576 | tf_op jit(solution)/shard_map/all_to_all | solution.py:61
  36.2 55.2 %reduce-scatter.5.cloned.1.call-start = ((), (), s32[]{:S(2)}) async-start(), calls=%async_computation.6 | async-start | bytes 2621440 | tf_op jit(solution)/shard_map/reduce_scatter | solution.py:78
  51.6 0.8 copy-start.1
  54.4 1.0 copy-start.3
  54.5 93.0 %reduce-scatter.3.cloned.1.call-start = ((), (), s32[]{:S(2)}) async-start(), calls=%async_computation.5 | async-start | bytes 5242880 | tf_op jit(solution)/shard_map/reduce_scatter | solution.py:69
  59.8 1.0 copy-start.2
Sparse Core Ops, SparseCore 0:
  54.6 36.8 reduce-scatter.4
  94.7 52.6 reduce-scatter.2
where the time goes:
time: 159 us; the launch traced here: 157 us
  waiting for transfers between devices  82.2 us (52%)
  matrix products  19.6 us (12%)
  blocking collectives  18.2 us (11%)
  between operations  14.1 us (9%)
  starting transfers between devices  12.6 us (8%)
  other arithmetic  7.47 us (5%)
  local copies, waits for them, and re-layouts  2.78 us (2%)
    reduce_scatter x1, waiting for transfers between devices, on_device(): lax.psum_scatter(lax.dot_general(columns, d_acts, (((0,), (0,)), ((), ())...  53.8 us
    all_to_all x1, blocking collectives, on_device(): lax.all_to_all(y_buf.reshape(n_experts, capacity, width), 'expert', split...  18.2 us
    reduce_scatter x1, waiting for transfers between devices, on_device(): lax.psum_scatter(lax.dot_general(columns, hidden, (((0,), (0,)), ((), ())...  10.7 us
    all_to_all x1, waiting for transfers between devices, on_device(): lax.all_to_all(send_x, 'expert', split_axis=0, concat_axis=0, tiled=True)  10.6 us
    all_to_all x1, waiting for transfers between devices, on_device(): lax.all_to_all(send_dy, 'expert', split_axis=0, concat_axis=0, tiled=True)  7.01 us
    all_to_all x1, starting transfers between devices, on_device(): lax.all_to_all(send_dy, 'expert', split_axis=0, concat_axis=0, tiled=True)  6.96 us
    all_to_all x1, starting transfers between devices, on_device(): lax.all_to_all(send_x, 'expert', split_axis=0, concat_axis=0, tiled=True)  5.64 us
    dot_general x1, matrix products, on_device(): acts = jnp.dot(x_buf, w_in[0], preferred_element_type=jnp.float32)  4.78 us
  transfers between devices with their start and end apart: 4, of which 4 were waited for; matrix products, arithmetic and copies ran while one was open for 9% of the time, Pallas kernels for 0%

commit v1 on v0

--- a/solution.py
+++ b/solution.py
@@ -1,7 +1,275 @@
+import functools
+
 import jax
 import jax.numpy as jnp
 from jax import lax
+from jax.experimental import pallas as pl
+from jax.experimental.pallas import tpu as pltpu
 from jax.sharding import PartitionSpec as P
+
+MESH = pl.DeviceIdType.MESH
+TILE = 256
+
+
+def fused_kernel(
+    n_exp, cap,
+    lat_ref, cot_ref, routes_ref, gates_ref, win_hbm, wout_hbm,
+    out_ref, gin_ref, gout_ref,
+    win, wout, sx, sdy, xall, dyall, a1, a2, hid, ybuf, back, place,
+    w_sem, zsend, zrecv, gsend, grecv,
+):
+    p = lax.axis_index("dp")
+    q = lax.axis_index("expert")
+    px, py = lax.rem(p, 2), lax.div(p, 2)
+    xn = (py * 2 + 1 - px, q)
+    yn = ((1 - py) * 2 + px, q)
+    tok, width = lat_ref.shape
+    rows = n_exp * cap
+    hidden = hid.shape[2]
+    share = gin_ref.shape[0]
+
+    def ahead(j):
+        return (p, lax.rem(q + j, n_exp))
+
+    def behind(j):
+        return (p, lax.rem(q + n_exp - j, n_exp))
+
+    barrier = pltpu.get_barrier_semaphore()
+    for j in range(1, n_exp):
+        pl.semaphore_signal(barrier, inc=1, device_id=ahead(j), device_id_type=MESH)
+    pl.semaphore_signal(barrier, inc=1, device_id=xn, device_id_type=MESH)
+    pl.semaphore_signal(barrier, inc=1, device_id=yn, device_id_type=MESH)
+    w_copies = (
+        pltpu.make_async_copy(win_hbm.at[0], win, w_sem.at[0]),
+        pltpu.make_async_copy(wout_hbm.at[0], wout, w_sem.at[1]),
+    )
+    for c in w_copies:
+        c.start()
+
+    rel = lax.rem(routes_ref[...] - q + n_exp, n_exp)
+    lane = lax.broadcasted_iota(jnp.int32, (tok, 128), 1)
+    onehot = jnp.where(rel == lane, 1.0, 0.0)
+    lower = jnp.where(
+        lax.broadcasted_iota(jnp.int32, (tok, tok), 1)
+        < lax.broadcasted_iota(jnp.int32, (tok, tok), 0),
+        1.0,
+        0.0,
+    )
+    before = jnp.dot(
+        lower.astype(jnp.bfloat16), onehot.astype(jnp.bfloat16), preferred_element_type=jnp.float32
+    )
+    slot = jnp.sum(before * onehot, axis=1, keepdims=True)
+    position = rel.astype(jnp.float32) * cap + slot
+    place[...] = jnp.where(
+        lax.broadcasted_iota(jnp.int32, (tok, rows), 1).astype(jnp.float32) == position, 1.0, 0.0
+    ).astype(jnp.bfloat16)
+
+    def placed(value):
+        return lax.dot_general(
+            place[...], value, (((0,), (0,)), ((), ())), preferred_element_type=jnp.float32
+        ).astype(jnp.bfloat16)
+
+    def part(j):
+        return pl.ds(j * cap, cap)
+
+    def z_copy(kind, src, dst, j, to):
+        return pltpu.make_async_remote_copy(
+            src_ref=src.at[part(j)],
+            dst_ref=dst.at[part(j)],
+            send_sem=zsend.at[kind, j],
+            recv_sem=zrecv.at[kind, j],
+            device_id=to,
+            device_id_type=MESH,
+        )
+
+    buffers = (xall, dyall)
+    z_copies = {}
+    far_first = sorted(range(1, n_exp), key=lambda j: -min(j, n_exp - j))
+    near_first = [0] + far_first[::-1]
+
+    placed_x = placed(lat_ref[...])
+    sx[...] = placed_x
+    xall[0, 0:cap, :] = placed_x[0:cap, :]
+    pl.semaphore_wait(barrier, n_exp + 1)
+    for j in far_first:
+        z_copies[0, j] = z_copy(0, sx, xall.at[0], j, ahead(j))
+        z_copies[0, j].start()
+    placed_dy = placed((gates_ref[...] * cot_ref[...].astype(jnp.float32)).astype(jnp.bfloat16))
+    sdy[...] = placed_dy
+    dyall[0, 0:cap, :] = placed_dy[0:cap, :]
+    for j in far_first:
+        z_copies[1, j] = z_copy(1, sdy, dyall.at[0], j, ahead(j))
+        z_copies[1, j].start()
+
+    g_copies = {}
+    received = set()
+
+    def g_copy(kind, src, dst, j, to):
+        c = pltpu.make_async_remote_copy(
+            src_ref=buffers[kind].at[src, part(j)],
+            dst_ref=buffers[kind].at[dst, part(j)],
+            send_sem=gsend.at[kind, dst - 1, j],
+            recv_sem=grecv.at[kind, dst - 1, j],
+            device_id=to,
+            device_id_type=MESH,
+        )
+        g_copies[kind, dst, j] = c
+        c.start()
+
+    def take(kind, group, j):
+        if (kind, group, j) not in received:
+            received.add((kind, group, j))
+            g_copies[kind, group, j].wait_recv()
+
+    def spread(kind, j):
+        if j:
+            z_copies[kind, j].wait_recv()
+        g_copy(kind, 0, 1, j, xn)
+        g_copy(kind, 0, 2, j, yn)
+
+    def relay(kind, i):
+        j = near_first[i]
+        if i % 2 == 0:
+            take(kind, 1, j)
+            g_copy(kind, 1, 3, j, yn)
+        else:
+            take(kind, 2, j)
+            g_copy(kind, 2, 3, j, xn)
+
+    def forward(r):
+        if r:
+            for j in near_first:
+                take(0, r, j)
+
+        @pl.loop(0, hidden // TILE)
+        def _(h):
+            lo = pl.ds(pl.multiple_of(h * TILE, TILE), TILE)
+            hi = pl.ds(pl.multiple_of(hidden + h * TILE, TILE), TILE)
+            gate = jnp.dot(xall[r], win[:, lo], preferred_element_type=jnp.float32)
+            upper = jnp.dot(xall[r], win[:, hi], preferred_element_type=jnp.float32)
+            sig = jax.nn.sigmoid(gate)
+            swish = gate * sig
+            hid[r, :, lo] = (swish * upper).astype(jnp.bfloat16)
+            a1[r, :, lo] = upper * sig * (1.0 + gate * (1.0 - sig))
+            a2[r, :, lo] = swish
+
+    def backward(r):
+        if r:
+            for j in near_first:
+                take(1, r, j)
+        cols = pl.ds(pl.multiple_of(p * share, share), share)
+
+        @pl.loop(0, hidden // TILE)
+        def _(h):
+            lo = pl.ds(pl.multiple_of(h * TILE, TILE), TILE)
+            hi = pl.ds(pl.multiple_of(hidden + h * TILE, TILE), TILE)
+            d_hid = jnp.dot(dyall[r], wout[:, lo], preferred_element_type=jnp.float32)
+            d_gate = (d_hid * a1[r, :, lo]).astype(jnp.bfloat16)
+            d_upper = (d_hid * a2[r, :, lo]).astype(jnp.bfloat16)
+
+            def add(ref, at, left, right):
+                term = lax.dot_general(
+                    left, right, (((0,), (0,)), ((), ())), preferred_element_type=jnp.float32
+                )
+                ref[:, at] = term if r == 0 else ref[:, at] + term
+
+            add(gin_ref, lo, xall[r, :, cols], d_gate)
+            add(gin_ref, hi, xall[r, :, cols], d_upper)
+            add(gout_ref, lo, dyall[r, :, cols], hid[r, :, lo])
+
+    lag = 2
+    for i, j in enumerate(near_first):
+        spread(0, j)
+        if i >= lag:
+            relay(0, i - lag)
+    for c in w_copies:
+        c.wait()
+    forward(0)
+
+    @pl.loop(0, width // TILE)
+    def _(l):
+        at = pl.ds(pl.multiple_of(l * TILE, TILE), TILE)
+        ybuf[:, at] = lax.dot_general(
+            hid[0], wout[at, :], (((1,), (1,)), ((), ())), preferred_element_type=jnp.float32
+        ).astype(jnp.bfloat16)
+
+    back[0:cap, :] = ybuf[0:cap, :]
+    for j in far_first:
+        z_copies[2, j] = z_copy(2, ybuf, back, j, behind(j))
+        z_copies[2, j].start()
+
+    for i in range(n_exp - lag, n_exp):
+        relay(0, i)
+    for i, j in enumerate(near_first):
+        spread(1, j)
+        if i >= lag:
+            relay(1, i - lag)
+        if i == n_exp // 2:
+            forward(1)
+    for i in range(n_exp - lag, n_exp):
+        relay(1, i)
+    forward(2)
+    backward(0)
+    forward(3)
+    backward(1)
+    backward(2)
+    for j in far_first:
+        z_copies[2, j].wait_recv()
+    out_ref[...] = (
+        gates_ref[...] * jnp.dot(place[...], back[...], preferred_element_type=jnp.float32)
+    ).astype(jnp.bfloat16)
+    backward(3)
+    for c in z_copies.values():
+        c.wait_send()
+    for c in g_copies.values():
+        c.wait_send()
+
+
+def fused(latent, cotangent, routes, gates, w_in, w_out, n_exp, cap):
+    tok, width = latent.shape
+    hidden = w_out.shape[2]
+    rows = n_exp * cap
+    share = width // 4
+    bf16, f32 = jnp.bfloat16, jnp.float32
+    vmem = pl.BlockSpec(memory_space=pltpu.VMEM)
+    hbm = pl.BlockSpec(memory_space=pl.ANY)
+    flops = 2 * rows * width * hidden * 16
+    output, grad_in, grad_out = pl.pallas_call(
+        functools.partial(fused_kernel, n_exp, cap),
+        out_shape=(
+            jax.ShapeDtypeStruct((tok, width), bf16),
+            jax.ShapeDtypeStruct((share, 2 * hidden), f32),
+            jax.ShapeDtypeStruct((share, hidden), f32),
+        ),
+        in_specs=[vmem, vmem, vmem, vmem, hbm, hbm],
+        out_specs=(vmem, vmem, vmem),
+        scratch_shapes=[
+            pltpu.VMEM((width, 2 * hidden), bf16),
+            pltpu.VMEM((width, hidden), bf16),
+            pltpu.VMEM((rows, width), bf16),
+            pltpu.VMEM((rows, width), bf16),
+            pltpu.VMEM((4, rows, width), bf16),
+            pltpu.VMEM((4, rows, width), bf16),
+            pltpu.VMEM((4, rows, hidden), f32),
+            pltpu.VMEM((4, rows, hidden), f32),
+            pltpu.VMEM((4, rows, hidden), bf16),
+            pltpu.VMEM((rows, width), bf16),
+            pltpu.VMEM((rows, width), bf16),
+            pltpu.VMEM((tok, rows), bf16),
+            pltpu.SemaphoreType.DMA((2,)),
+            pltpu.SemaphoreType.DMA((3, n_exp)),
+            pltpu.SemaphoreType.DMA((3, n_exp)),
+            pltpu.SemaphoreType.DMA((2, 3, n_exp)),
+            pltpu.SemaphoreType.DMA((2, 3, n_exp)),
+        ],
+        compiler_params=pltpu.CompilerParams(
+            collective_id=0, has_side_effects=True, vmem_limit_bytes=48 * 1024 * 1024
+        ),
+        cost_estimate=pl.CostEstimate(
+            flops=flops, bytes_accessed=10 * 1024 * 1024, transcendentals=4 * rows * hidden
+        ),
+    )(latent, cotangent, routes, gates, w_in, w_out)
+    return output, grad_in.reshape(1, share, 2 * hidden), grad_out.reshape(1, share, hidden)
 
 
 def on_device(latent, cotangent, routes, gates, w_in, w_out):
@@ -12,6 +280,8 @@
     width = latent.shape[1]
     hidden_units = w_out.shape[2]
     capacity = max(2, 2 * tok_count * top_count // n_experts)
+    if n_replicas == 4 and top_count == 1 and capacity % 16 == 0 and tok_count == 128:
+        return fused(latent, cotangent, routes, gates, w_in, w_out, n_experts, capacity)
     route_flat = routes.reshape(-1)
     gate_flat = gates.reshape(-1)
     onehot = (route_flat[:, None] == jnp.arange(n_experts, dtype=jnp.int32)[None, :]).astype(

time: 159 us -> 78.2 us (0.49)
  waiting for transfers between devices: 82.2 us -> 0 us
  Pallas kernels: 0 us -> 69 us
  matrix products: 19.6 us -> 0 us
  blocking collectives: 18.2 us -> 0 us
  between operations: 14.1 us -> 0.65 us
  starting transfers between devices: 12.6 us -> 0 us
  other arithmetic: 7.47 us -> 0 us
  local copies, waits for them, and re-layouts: 2.78 us -> 8 us
    pallas_call x0 -> x1, Pallas kernels: none -> 69 us  [fused(): pl.pallas_call(functools.partial(fused_kernel, n_exp, cap), out_shape=(ja...]
    reduce_scatter x2 -> x0, waiting for transfers between devices: 64.5 us -> none  [the longest x1 53.8 us: on_device(): lax.psum_scatter(lax.dot_general(columns, d_acts, (((0,), (0,)), ((), ())...]
    dot_general x8 -> x0, matrix products: 19.6 us -> none  [the longest x1 4.78 us: on_device(): acts = jnp.dot(x_buf, w_in[0], preferred_element_type=jnp.float32)]
    all_to_all x1 -> x0, blocking collectives: 18.2 us -> none  [on_device(): lax.all_to_all(y_buf.reshape(n_experts, capacity, width), 'expert', split...]
    all_to_all x2 -> x0, waiting for transfers between devices: 17.6 us -> none  [the longest x1 10.6 us: on_device(): lax.all_to_all(send_x, 'expert', split_axis=0, concat_axis=0, tiled=True)]
    all_to_all x2 -> x0, starting transfers between devices: 12.6 us -> none  [the longest x1 6.96 us: on_device(): lax.all_to_all(send_dy, 'expert', split_axis=0, concat_axis=0, tiled=True)]
    unnamed x12 -> x11, local copies, waits for them, and re-layouts: 2.78 us -> 8 us
    reshape x2 -> x0, other arithmetic: 4.91 us -> none  [the longest x1 2.79 us: on_device(): grad_in.reshape(1, share, 2 * hidden_units)]
  transfers between devices with their start and end apart: 4 -> 0, of which waited for: 4 -> 0; matrix products, arithmetic and copies ran while one was open for 9% -> 0% of each run, Pallas kernels for 0% -> 0%
where the time goes in v1:
time: 78.2 us; the launch traced here: 77.6 us
  Pallas kernels  69 us (88%)
  local copies, waits for them, and re-layouts  8 us (10%)
    pallas_call x1, Pallas kernels, fused(): pl.pallas_call(functools.partial(fused_kernel, n_exp, cap), out_shape=(ja...  69 us
    unnamed x11, local copies, waits for them, and re-layouts  8 us

profile of v1, /device:TPU:9, one launch (start us, length us, event | category | flops | bytes accessed | tf_op | source)
XLA Modules:
  0.0 77.6 jit_solution(15425053496896666310)
XLA Ops:
  0.6 0.8 copy.9.routes_ref
  1.4 0.8 copy.10.gates_ref
  2.2 0.0 copy-start
  2.2 1.6 %copy-done = bf16[1,1024,1024]{2,1,0:T(8,128)(2,1)S(1)} copy-done((bf16[1,1024,1024]{2,1,0:T(8,128)(2,1)S(1)}, bf16[1,1024,1024]{2,1,0:T(8,128)(2,1)}, u32[]{:S(2)}) %copy-start) | copy-done | bytes 2097176
  3.7 0.0 copy-start.1
  3.7 0.9 %copy-done.1 = bf16[128,1024]{1,0:T(8,128)(2,1)S(1)} copy-done((bf16[128,1024]{1,0:T(8,128)(2,1)S(1)}, bf16[128,1024]{1,0:T(8,128)(2,1)}, u32[]{:S(2)}) %copy-start.1) | copy-done | bytes 262168
  4.7 0.0 copy-start.2
  4.7 0.9 %copy-done.2 = bf16[128,1024]{1,0:T(8,128)(2,1)S(1)} copy-done((bf16[128,1024]{1,0:T(8,128)(2,1)S(1)}, bf16[128,1024]{1,0:T(8,128)(2,1)}, u32[]{:S(2)}) %copy-start.2) | copy-done | bytes 262168
  5.6 69.0 %shard_map.85 = (bf16[128,1024]{1,0:T(8,128)(2,1)S(1)}, f32[256,2048]{1,0:T(8,128)S(1)}, f32[256,1024]{1,0:T(8,128)S(1)}) custom-call(bf16[128,1024]{1,0:T(8,128)(2,1)S(1)} %copy-done.1, bf16[128,1024]{1,0:T(8,128)(2,1)S(1)} %copy-done.2, s32[128,1]{1,0:T(8,128)S(1)} %copy.9.routes_ref, f32[128,1]{1,0:T(8,128)S(1)} %copy.10.gates_ref, ...), custom_call_target="tpu_custom_call" | custom-call | flops 8589934592 | bytes 10485760 | tf_op jit(solution)/shard_map/pallas_call | solution.py:237
  74.7 0.7 copy.14
  75.4 1.3 %copy.15 = f32[1,256,2048]{2,1,0:T(8,128)} copy(f32[1,256,2048]{2,1,0:T(8,128)S(1)} %bitcast.2) | data formatting | bytes 4194304
  76.7 1.0 %copy.16 = f32[1,256,1024]{2,1,0:T(8,128)} copy(f32[1,256,1024]{2,1,0:T(8,128)S(1)} %bitcast.3) | data formatting | bytes 2097152
Async XLA Ops:
  2.2 1.6 %copy-start = (bf16[1,1024,1024]{2,1,0:T(8,128)(2,1)S(1)}, bf16[1,1024,1024]{2,1,0:T(8,128)(2,1)}, u32[]{:S(2)}) copy-start(bf16[1,1024,1024]{2,1,0:T(8,128)(2,1)} %wout_hbm.1) | copy-start | bytes 6291460
  3.7 0.9 %copy-start.1 = (bf16[128,1024]{1,0:T(8,128)(2,1)S(1)}, bf16[128,1024]{1,0:T(8,128)(2,1)}, u32[]{:S(2)}) copy-start(bf16[128,1024]{1,0:T(8,128)(2,1)} %lat_ref.1) | copy-start | bytes 786436
  4.7 0.9 %copy-start.2 = (bf16[128,1024]{1,0:T(8,128)(2,1)S(1)}, bf16[128,1024]{1,0:T(8,128)(2,1)}, u32[]{:S(2)}) copy-start(bf16[128,1024]{1,0:T(8,128)(2,1)} %cot_ref.1) | copy-start | bytes 786436

commit v2 on v0

--- a/solution.py
+++ b/solution.py
@@ -1,7 +1,315 @@
+import functools
+
 import jax
 import jax.numpy as jnp
 from jax import lax
+from jax.experimental import pallas as pl
+from jax.experimental.pallas import tpu as pltpu
 from jax.sharding import PartitionSpec as P
+
+MESH = pl.DeviceIdType.MESH
+TILE = 256
+
+
+def fused_kernel(
+    n_exp, cap,
+    lat_hbm, cot_hbm, routes_ref, gates_ref, win_hbm, wout_hbm,
+    out_ref, gin_ref, gout_ref,
+    lat, cot, win, wout, sx, sdy, xall, dyall, a1, a2, hid, ybuf, back, place,
+    in_sem, zsend, zrecv, gsend, grecv,
+):
+    p = lax.axis_index("dp")
+    q = lax.axis_index("expert")
+    px, py = lax.rem(p, 2), lax.div(p, 2)
+    xn = (py * 2 + 1 - px, q)
+    yn = ((1 - py) * 2 + px, q)
+    tok, width = lat.shape
+    rows = n_exp * cap
+    hidden = hid.shape[2]
+    share = gin_ref.shape[0]
+    half = n_exp // 2
+    order = sorted(range(n_exp), key=lambda j: (min(j, n_exp - j), j))
+    far_first = list(range(1, n_exp))[::-1]
+
+    def ahead(i):
+        return (p, lax.rem(q + order[i], n_exp))
+
+    def behind(i):
+        return (p, lax.rem(q + n_exp - order[i], n_exp))
+
+    barrier = pltpu.get_barrier_semaphore()
+    for i in range(1, n_exp):
+        pl.semaphore_signal(barrier, inc=1, device_id=ahead(i), device_id_type=MESH)
+    pl.semaphore_signal(barrier, inc=1, device_id=xn, device_id_type=MESH)
+    pl.semaphore_signal(barrier, inc=1, device_id=yn, device_id_type=MESH)
+    loads = [
+        pltpu.make_async_copy(src, dst, in_sem.at[n])
+        for n, (src, dst) in enumerate(
+            ((lat_hbm, lat), (cot_hbm, cot), (win_hbm.at[0], win), (wout_hbm.at[0], wout))
+        )
+    ]
+    for c in loads:
+        c.start()
+
+    rel = lax.rem(routes_ref[...] - q + n_exp, n_exp)
+    index = jnp.zeros_like(rel)
+    for i, j in enumerate(order):
+        index = jnp.where(rel == j, i, index)
+    i0 = lax.broadcasted_iota(jnp.int32, (tok, tok), 0)
+    i1 = lax.broadcasted_iota(jnp.int32, (tok, tok), 1)
+    onehot = jnp.where(i0 == index, 1.0, 0.0)
+    earlier = jnp.where(i0 < i1, 1.0, 0.0)
+    before = jnp.dot(
+        onehot.astype(jnp.bfloat16), earlier.astype(jnp.bfloat16), preferred_element_type=jnp.float32
+    )
+    slot = jnp.sum(before * onehot, axis=0, keepdims=True)
+    position = index.astype(jnp.float32) * cap + slot
+    place[...] = jnp.where(
+        lax.broadcasted_iota(jnp.int32, (rows, tok), 0).astype(jnp.float32) == position, 1.0, 0.0
+    ).astype(jnp.bfloat16)
+    gates = jnp.sum(jnp.where(i0 == i1, gates_ref[...], 0.0), axis=1, keepdims=True)
+
+    def place_rows(value, sent, kept):
+        placed = jnp.dot(place[...], value, preferred_element_type=jnp.float32).astype(jnp.bfloat16)
+        sent[...] = placed
+        kept[0, 0:cap, :] = placed[0:cap, :]
+
+    def at(buf, group, i):
+        return buf.at[(i // half) * 2 + group // 2, pl.ds((group % 2) * (rows // 2) + (i % half) * cap, cap)]
+
+    def slots(i):
+        return pl.ds(i * cap, cap)
+
+    def z_copy(kind, src, dst, i, to):
+        c = pltpu.make_async_remote_copy(
+            src_ref=src.at[slots(i)],
+            dst_ref=dst,
+            send_sem=zsend.at[kind, i],
+            recv_sem=zrecv.at[kind, i],
+            device_id=to,
+            device_id_type=MESH,
+        )
+        z_copies[kind, i] = c
+        c.start()
+
+    buffers = (xall, dyall)
+    z_copies, g_copies = {}, {}
+    received = set()
+
+    loads[0].wait()
+    place_rows(lat[...], sx, xall)
+    pl.semaphore_wait(barrier, n_exp + 1)
+    for i in far_first:
+        z_copy(0, sx, at(xall, 0, i), i, ahead(i))
+
+    def g_copy(kind, src, dst, i, to):
+        c = pltpu.make_async_remote_copy(
+            src_ref=at(buffers[kind], src, i),
+            dst_ref=at(buffers[kind], dst, i),
+            send_sem=gsend.at[kind, dst - 1, i],
+            recv_sem=grecv.at[kind, dst - 1, i],
+            device_id=to,
+            device_id_type=MESH,
+        )
+        g_copies[kind, dst, i] = c
+        c.start()
+
+    def take(kind, group, i):
+        if (kind, group, i) not in received:
+            received.add((kind, group, i))
+            if group:
+                g_copies[kind, group, i].wait_recv()
+            elif i:
+                z_copies[kind, i].wait_recv()
+
+    def spread(kind, i):
+        take(kind, 0, i)
+        g_copy(kind, 0, 1, i, xn)
+        g_copy(kind, 0, 2, i, yn)
+
+    def relay(kind, i):
+        if i % 2 == 0:
+            take(kind, 1, i)
+            g_copy(kind, 1, 3, i, yn)
+        else:
+            take(kind, 2, i)
+            g_copy(kind, 2, 3, i, xn)
+
+    def take_chunk(kind, c):
+        for i in range(half):
+            take(kind, c % 2 * 2, c // 2 * half + i)
+            take(kind, c % 2 * 2 + 1, c // 2 * half + i)
+
+    def forward(c):
+        take_chunk(0, c)
+
+        @pl.loop(0, hidden // TILE)
+        def _(h):
+            lo = pl.ds(pl.multiple_of(h * TILE, TILE), TILE)
+            hi = pl.ds(pl.multiple_of(hidden + h * TILE, TILE), TILE)
+            gate = jnp.dot(xall[c], win[:, lo], preferred_element_type=jnp.float32)
+            upper = jnp.dot(xall[c], win[:, hi], preferred_element_type=jnp.float32)
+            sig = jax.nn.sigmoid(gate)
+            swish = gate * sig
+            hid[c, :, lo] = (swish * upper).astype(jnp.bfloat16)
+            a1[c, :, lo] = upper * sig * (1.0 + gate * (1.0 - sig))
+            a2[c, :, lo] = swish
+
+    def backward(c):
+        take_chunk(1, c)
+        cols = pl.ds(pl.multiple_of(p * share, share), share)
+
+        @pl.loop(0, hidden // TILE)
+        def _(h):
+            lo = pl.ds(pl.multiple_of(h * TILE, TILE), TILE)
+            hi = pl.ds(pl.multiple_of(hidden + h * TILE, TILE), TILE)
+            d_hid = jnp.dot(dyall[c], wout[:, lo], preferred_element_type=jnp.float32)
+            d_gate = (d_hid * a1[c, :, lo]).astype(jnp.bfloat16)
+            d_upper = (d_hid * a2[c, :, lo]).astype(jnp.bfloat16)
+
+            def add(ref, where, left, right):
+                term = lax.dot_general(
+                    left, right, (((0,), (0,)), ((), ())), preferred_element_type=jnp.float32
+                )
+                ref[:, where] = term if c == 0 else ref[:, where] + term
+
+            add(gin_ref, lo, xall[c, :, cols], d_gate)
+            add(gin_ref, hi, xall[c, :, cols], d_upper)
+            add(gout_ref, lo, dyall[c, :, cols], hid[c, :, lo])
+
+    def expert_out():
+        @pl.loop(0, width // TILE)
+        def _(l):
+            tile = pl.ds(pl.multiple_of(l * TILE, TILE), TILE)
+            own = jnp.concatenate([hid[0, 0 : rows // 2, :], hid[2, 0 : rows // 2, :]], axis=0)
+            ybuf[:, tile] = lax.dot_general(
+                own, wout[tile, :], (((1,), (1,)), ((), ())), preferred_element_type=jnp.float32
+            ).astype(jnp.bfloat16)
+
+        back[0:cap, :] = ybuf[0:cap, :]
+
+    spread(0, 0)
+    loads[1].wait()
+    place_rows((gates * cot[...].astype(jnp.float32)).astype(jnp.bfloat16), sdy, dyall)
+    for i in range(1, n_exp):
+        spread(0, i)
+        k = far_first[i - 1]
+        z_copy(1, sdy, at(dyall, 0, k), k, ahead(k))
+        if i >= 2:
+            relay(0, i - 2)
+    spread(1, 0)
+    spread(1, 1)
+    loads[2].wait()
+    loads[3].wait()
+    forward(0)
+    relay(0, n_exp - 2)
+    relay(0, n_exp - 1)
+    spread(1, 2)
+    relay(1, 0)
+    forward(2)
+    expert_out()
+    spread(1, 3)
+    relay(1, 1)
+    for i in far_first:
+        z_copy(2, ybuf, back.at[slots(i)], i, behind(i))
+    forward(1)
+    spread(1, 4)
+    relay(1, 2)
+    forward(3)
+    spread(1, 5)
+    relay(1, 3)
+    backward(0)
+    spread(1, 6)
+    relay(1, 4)
+    spread(1, 7)
+    relay(1, 5)
+    backward(1)
+    relay(1, 6)
+    relay(1, 7)
+    backward(2)
+    for i in far_first:
+        z_copies[2, i].wait_recv()
+    out_ref[...] = (
+        gates
+        * lax.dot_general(
+            place[...], back[...], (((0,), (0,)), ((), ())), preferred_element_type=jnp.float32
+        )
+    ).astype(jnp.bfloat16)
+    backward(3)
+    for c in z_copies.values():
+        c.wait_send()
+    for c in g_copies.values():
+        c.wait_send()
+
+
+def store_kernel(*refs):
+    count = len(refs) // 2
+    copies = [
+        pltpu.make_async_copy(refs[n], refs[count + n], refs[-1].at[n]) for n in range(count)
+    ]
+    for c in copies:
+        c.start()
+    for c in copies:
+        c.wait()
+
+
+def fused(latent, cotangent, routes, gates, w_in, w_out, n_exp, cap):
+    tok, width = latent.shape
+    hidden = w_out.shape[2]
+    rows = n_exp * cap
+    share = width // 4
+    bf16, f32 = jnp.bfloat16, jnp.float32
+    vmem = pl.BlockSpec(memory_space=pltpu.VMEM)
+    hbm = pl.BlockSpec(memory_space=pltpu.HBM)
+    anywhere = pl.BlockSpec(memory_space=pl.ANY)
+    flops = 2 * rows * width * hidden * 16
+    shapes = (
+        jax.ShapeDtypeStruct((tok, width), bf16),
+        jax.ShapeDtypeStruct((share, 2 * hidden), f32),
+        jax.ShapeDtypeStruct((share, hidden), f32),
+    )
+    results = pl.pallas_call(
+        functools.partial(fused_kernel, n_exp, cap),
+        out_shape=shapes,
+        in_specs=[hbm, hbm, vmem, vmem, hbm, hbm],
+        out_specs=(vmem, vmem, vmem),
+        scratch_shapes=[
+            pltpu.VMEM((tok, width), bf16),
+            pltpu.VMEM((tok, width), bf16),
+            pltpu.VMEM((width, 2 * hidden), bf16),
+            pltpu.VMEM((width, hidden), bf16),
+            pltpu.VMEM((rows, width), bf16),
+            pltpu.VMEM((rows, width), bf16),
+            pltpu.VMEM((4, rows, width), bf16),
+            pltpu.VMEM((4, rows, width), bf16),
+            pltpu.VMEM((4, rows, hidden), f32),
+            pltpu.VMEM((4, rows, hidden), f32),
+            pltpu.VMEM((4, rows, hidden), bf16),
+            pltpu.VMEM((rows, width), bf16),
+            pltpu.VMEM((rows, width), bf16),
+            pltpu.VMEM((rows, tok), bf16),
+            pltpu.SemaphoreType.DMA((4,)),
+            pltpu.SemaphoreType.DMA((3, n_exp)),
+            pltpu.SemaphoreType.DMA((3, n_exp)),
+            pltpu.SemaphoreType.DMA((2, 3, n_exp)),
+            pltpu.SemaphoreType.DMA((2, 3, n_exp)),
+        ],
+        compiler_params=pltpu.CompilerParams(
+            collective_id=0, has_side_effects=True, vmem_limit_bytes=48 * 1024 * 1024
+        ),
+        cost_estimate=pl.CostEstimate(
+            flops=flops, bytes_accessed=10 * 1024 * 1024, transcendentals=4 * rows * hidden
+        ),
+    )(latent, cotangent, routes.reshape(1, tok), gates.reshape(1, tok), w_in, w_out)
+    output, grad_in, grad_out = pl.pallas_call(
+        store_kernel,
+        out_shape=shapes,
+        in_specs=[anywhere] * 3,
+        out_specs=(hbm, hbm, hbm),
+        scratch_shapes=[pltpu.SemaphoreType.DMA((3,))],
+        cost_estimate=pl.CostEstimate(flops=0, bytes_accessed=7 * 1024 * 1024, transcendentals=0),
+    )(*results)
+    return output, grad_in.reshape(1, share, 2 * hidden), grad_out.reshape(1, share, hidden)
 
 
 def on_device(latent, cotangent, routes, gates, w_in, w_out):
@@ -12,6 +320,8 @@
     width = latent.shape[1]
     hidden_units = w_out.shape[2]
     capacity = max(2, 2 * tok_count * top_count // n_experts)
+    if n_replicas == 4 and top_count == 1 and capacity % 16 == 0 and tok_count == 128 and n_experts == 8:
+        return fused(latent, cotangent, routes, gates, w_in, w_out, n_experts, capacity)
     route_flat = routes.reshape(-1)
     gate_flat = gates.reshape(-1)
     onehot = (route_flat[:, None] == jnp.arange(n_experts, dtype=jnp.int32)[None, :]).astype(

time: 159 us -> 172 us (1.082)
  Pallas kernels: 0 us -> 162 us
  waiting for transfers between devices: 82.2 us -> 0 us
  matrix products: 19.6 us -> 0 us
  blocking collectives: 18.2 us -> 0 us
  between operations: 14.1 us -> 0.66 us
  starting transfers between devices: 12.6 us -> 0 us
  other arithmetic: 7.47 us -> 0 us
  local copies, waits for them, and re-layouts: 2.78 us -> 7.81 us
    pallas_call x0 -> x2, Pallas kernels: none -> 162 us  [the longest x1 104 us: fused(): pl.pallas_call(store_kernel, out_shape=shapes, in_specs=[anywhere] * 3, o...]
    reduce_scatter x2 -> x0, waiting for transfers between devices: 64.5 us -> none  [the longest x1 53.8 us: on_device(): lax.psum_scatter(lax.dot_general(columns, d_acts, (((0,), (0,)), ((), ())...]
    dot_general x8 -> x0, matrix products: 19.6 us -> none  [the longest x1 4.78 us: on_device(): acts = jnp.dot(x_buf, w_in[0], preferred_element_type=jnp.float32)]
    all_to_all x1 -> x0, blocking collectives: 18.2 us -> none  [on_device(): lax.all_to_all(y_buf.reshape(n_experts, capacity, width), 'expert', split...]
    all_to_all x2 -> x0, waiting for transfers between devices: 17.6 us -> none  [the longest x1 10.6 us: on_device(): lax.all_to_all(send_x, 'expert', split_axis=0, concat_axis=0, tiled=True)]
    all_to_all x2 -> x0, starting transfers between devices: 12.6 us -> none  [the longest x1 6.96 us: on_device(): lax.all_to_all(send_dy, 'expert', split_axis=0, concat_axis=0, tiled=True)]
    unnamed x12 -> x16, local copies, waits for them, and re-layouts: 2.78 us -> 7.81 us
    reshape x2 -> x0, other arithmetic: 4.91 us -> none  [the longest x1 2.79 us: on_device(): grad_in.reshape(1, share, 2 * hidden_units)]
  transfers between devices with their start and end apart: 4 -> 0, of which waited for: 4 -> 0; matrix products, arithmetic and copies ran while one was open for 9% -> 0% of each run, Pallas kernels for 0% -> 0%
where the time goes in v2:
time: 172 us; the launch traced here: 170 us
  Pallas kernels  162 us (94%)
  local copies, waits for them, and re-layouts  7.81 us (5%)
    pallas_call x1, Pallas kernels, fused(): pl.pallas_call(store_kernel, out_shape=shapes, in_specs=[anywhere] * 3, o...  104 us
    pallas_call x1, Pallas kernels, fused(): pl.pallas_call(functools.partial(fused_kernel, n_exp, cap), out_shape=sha...  57.3 us
    unnamed x16, local copies, waits for them, and re-layouts  7.81 us

profile of v2, /device:TPU:9, one launch (start us, length us, event | category | flops | bytes accessed | tf_op | source)
XLA Modules:
  0.0 170.1 jit_solution(12282683978462660510)
XLA Ops:
  0.6 0.0 copy-start.3
  0.6 1.6 copy-done.3
  2.2 0.0 copy-start.4
  2.2 0.9 copy-done.4
  3.2 0.0 copy-start.5
  3.2 0.9 copy-done.5
  4.1 0.0 copy-start.6
  4.1 0.7 copy-done.6
  4.8 0.0 copy-start.7
  4.8 0.7 copy-done.7
  5.4 57.3 %shard_map.85 = (bf16[128,1024]{1,0:T(8,128)(2,1)S(1)}, f32[256,2048]{1,0:T(8,128)S(1)}, f32[256,1024]{1,0:T(8,128)S(1)}) custom-call(bf16[128,1024]{1,0:T(8,128)(2,1)S(1)} %copy-done.4, bf16[128,1024]{1,0:T(8,128)(2,1)S(1)} %copy-done.5, s32[1,128]{1,0:T(1,128)S(1)} %bitcast.4, f32[1,128]{1,0:T(1,128)S(1)} %bitcast.5, bf16[1,1024,2048]{2,1,0:T(8,128)(2,1)} %win_hbm.1, ...), custom_call_target="tpu_custom_call" | custom-call | flops 8589934592 | bytes 10485760 | tf_op jit(solution)/shard_map/pallas_call | solution.py:271
  62.8 0.0 copy-start
  62.8 1.3 copy-done
  64.1 0.0 copy-start.1
  64.1 1.0 copy-done.1
  65.1 0.0 copy-start.2
  65.1 0.7 copy-done.2
  65.8 104.4 %shard_map.86 = (bf16[128,1024]{1,0:T(8,128)(2,1)}, f32[256,2048]{1,0:T(8,128)}, f32[256,1024]{1,0:T(8,128)}) custom-call(bf16[128,1024]{1,0:T(8,128)(2,1)} %copy-done.2, f32[256,2048]{1,0:T(8,128)} %copy-done, f32[256,1024]{1,0:T(8,128)} %copy-done.1), custom_call_target="tpu_custom_call" | custom-call | bytes 7340032 | tf_op jit(solution)/shard_map/pallas_call | solution.py:304
Async XLA Ops:
  0.6 1.6 copy-start.3
  2.2 0.9 copy-start.4
  3.2 0.9 copy-start.5
  4.1 0.7 copy-start.6
  4.8 0.7 copy-start.7
  62.8 1.3 copy-start
  64.1 1.0 copy-start.1
  65.1 0.7 copy-start.2

commit v3 on v2

--- a/solution.py
+++ b/solution.py
@@ -14,9 +14,9 @@
 def fused_kernel(
     n_exp, cap,
     lat_hbm, cot_hbm, routes_ref, gates_ref, win_hbm, wout_hbm,
-    out_ref, gin_ref, gout_ref,
-    lat, cot, win, wout, sx, sdy, xall, dyall, a1, a2, hid, ybuf, back, place,
-    in_sem, zsend, zrecv, gsend, grecv,
+    out_hbm, gin_hbm, gout_hbm,
+    out, gin, gout, lat, cot, win, wout, sx, sdy, xall, dyall, a1, a2, hid, ybuf, back, place,
+    in_sem, out_sem, zsend, zrecv, gsend, grecv,
 ):
     p = lax.axis_index("dp")
     q = lax.axis_index("expert")
@@ -26,7 +26,7 @@
     tok, width = lat.shape
     rows = n_exp * cap
     hidden = hid.shape[2]
-    share = gin_ref.shape[0]
+    share = gin.shape[0]
     half = n_exp // 2
     order = sorted(range(n_exp), key=lambda j: (min(j, n_exp - j), j))
     far_first = list(range(1, n_exp))[::-1]
@@ -75,7 +75,9 @@
         kept[0, 0:cap, :] = placed[0:cap, :]
 
     def at(buf, group, i):
-        return buf.at[(i // half) * 2 + group // 2, pl.ds((group % 2) * (rows // 2) + (i % half) * cap, cap)]
+        if group in (0, 3):
+            return buf.at[group, pl.ds(i * cap, cap)]
+        return buf.at[1 + i // half, pl.ds((group - 1) * (rows // 2) + (i % half) * cap, cap)]
 
     def slots(i):
         return pl.ds(i * cap, cap)
@@ -136,9 +138,13 @@
             g_copy(kind, 2, 3, i, xn)
 
     def take_chunk(kind, c):
-        for i in range(half):
-            take(kind, c % 2 * 2, c // 2 * half + i)
-            take(kind, c % 2 * 2 + 1, c // 2 * half + i)
+        if c in (0, 3):
+            for i in range(n_exp):
+                take(kind, c, i)
+        else:
+            for i in range((c - 1) * half, c * half):
+                take(kind, 1, i)
+                take(kind, 2, i)
 
     def forward(c):
         take_chunk(0, c)
@@ -173,17 +179,28 @@
                 )
                 ref[:, where] = term if c == 0 else ref[:, where] + term
 
-            add(gin_ref, lo, xall[c, :, cols], d_gate)
-            add(gin_ref, hi, xall[c, :, cols], d_upper)
-            add(gout_ref, lo, dyall[c, :, cols], hid[c, :, lo])
+            add(gin, lo, xall[c, :, cols], d_gate)
+            add(gin, hi, xall[c, :, cols], d_upper)
+            add(gout, lo, dyall[c, :, cols], hid[c, :, lo])
+            if c == 3:
+                for copy in stores(h):
+                    copy.start()
+
+    def stores(h):
+        lo = pl.ds(pl.multiple_of(h * TILE, TILE), TILE)
+        hi = pl.ds(pl.multiple_of(hidden + h * TILE, TILE), TILE)
+        pairs = ((gin, gin_hbm, lo), (gin, gin_hbm, hi), (gout, gout_hbm, lo))
+        return [
+            pltpu.make_async_copy(src.at[:, where], dst.at[:, where], out_sem.at[n, h])
+            for n, (src, dst, where) in enumerate(pairs)
+        ]
 
     def expert_out():
         @pl.loop(0, width // TILE)
         def _(l):
             tile = pl.ds(pl.multiple_of(l * TILE, TILE), TILE)
-            own = jnp.concatenate([hid[0, 0 : rows // 2, :], hid[2, 0 : rows // 2, :]], axis=0)
             ybuf[:, tile] = lax.dot_general(
-                own, wout[tile, :], (((1,), (1,)), ((), ())), preferred_element_type=jnp.float32
+                hid[0], wout[tile, :], (((1,), (1,)), ((), ())), preferred_element_type=jnp.float32
             ).astype(jnp.bfloat16)
 
         back[0:cap, :] = ybuf[0:cap, :]
@@ -193,64 +210,57 @@
     place_rows((gates * cot[...].astype(jnp.float32)).astype(jnp.bfloat16), sdy, dyall)
     for i in range(1, n_exp):
         spread(0, i)
-        k = far_first[i - 1]
+        k = ([1] + far_first[:-1])[i - 1]
         z_copy(1, sdy, at(dyall, 0, k), k, ahead(k))
-        if i >= 2:
-            relay(0, i - 2)
     spread(1, 0)
     spread(1, 1)
     loads[2].wait()
     loads[3].wait()
     forward(0)
-    relay(0, n_exp - 2)
-    relay(0, n_exp - 1)
-    spread(1, 2)
-    relay(1, 0)
-    forward(2)
     expert_out()
-    spread(1, 3)
-    relay(1, 1)
     for i in far_first:
         z_copy(2, ybuf, back.at[slots(i)], i, behind(i))
+    for i in range(n_exp):
+        relay(0, i)
+    spread(1, 2)
+    spread(1, 3)
+    relay(1, 0)
     forward(1)
     spread(1, 4)
+    relay(1, 1)
+    forward(2)
+    spread(1, 5)
     relay(1, 2)
+    relay(1, 3)
     forward(3)
-    spread(1, 5)
-    relay(1, 3)
+    spread(1, 6)
+    spread(1, 7)
+    relay(1, 4)
+    relay(1, 5)
     backward(0)
-    spread(1, 6)
-    relay(1, 4)
-    spread(1, 7)
-    relay(1, 5)
-    backward(1)
     relay(1, 6)
     relay(1, 7)
+    backward(1)
     backward(2)
     for i in far_first:
         z_copies[2, i].wait_recv()
-    out_ref[...] = (
+    out[...] = (
         gates
         * lax.dot_general(
             place[...], back[...], (((0,), (0,)), ((), ())), preferred_element_type=jnp.float32
         )
     ).astype(jnp.bfloat16)
+    out_copy = pltpu.make_async_copy(out, out_hbm, in_sem.at[4])
+    out_copy.start()
     backward(3)
     for c in z_copies.values():
         c.wait_send()
     for c in g_copies.values():
         c.wait_send()
-
-
-def store_kernel(*refs):
-    count = len(refs) // 2
-    copies = [
-        pltpu.make_async_copy(refs[n], refs[count + n], refs[-1].at[n]) for n in range(count)
-    ]
-    for c in copies:
-        c.start()
-    for c in copies:
-        c.wait()
+    out_copy.wait()
+    for h in range(hidden // TILE):
+        for c in stores(h):
+            c.wait()
 
 
 def fused(latent, cotangent, routes, gates, w_in, w_out, n_exp, cap):
@@ -261,19 +271,21 @@
     bf16, f32 = jnp.bfloat16, jnp.float32
     vmem = pl.BlockSpec(memory_space=pltpu.VMEM)
     hbm = pl.BlockSpec(memory_space=pltpu.HBM)
-    anywhere = pl.BlockSpec(memory_space=pl.ANY)
     flops = 2 * rows * width * hidden * 16
     shapes = (
         jax.ShapeDtypeStruct((tok, width), bf16),
         jax.ShapeDtypeStruct((share, 2 * hidden), f32),
         jax.ShapeDtypeStruct((share, hidden), f32),
     )
-    results = pl.pallas_call(
+    output, grad_in, grad_out = pl.pallas_call(
         functools.partial(fused_kernel, n_exp, cap),
         out_shape=shapes,
         in_specs=[hbm, hbm, vmem, vmem, hbm, hbm],
-        out_specs=(vmem, vmem, vmem),
+        out_specs=(hbm, hbm, hbm),
         scratch_shapes=[
+            pltpu.VMEM((tok, width), bf16),
+            pltpu.VMEM((share, 2 * hidden), f32),
+            pltpu.VMEM((share, hidden), f32),
             pltpu.VMEM((tok, width), bf16),
             pltpu.VMEM((tok, width), bf16),
             pltpu.VMEM((width, 2 * hidden), bf16),
@@ -288,27 +300,20 @@
             pltpu.VMEM((rows, width), bf16),
             pltpu.VMEM((rows, width), bf16),
             pltpu.VMEM((rows, tok), bf16),
-            pltpu.SemaphoreType.DMA((4,)),
+            pltpu.SemaphoreType.DMA((5,)),
+            pltpu.SemaphoreType.DMA((3, hidden // TILE)),
             pltpu.SemaphoreType.DMA((3, n_exp)),
             pltpu.SemaphoreType.DMA((3, n_exp)),
             pltpu.SemaphoreType.DMA((2, 3, n_exp)),
             pltpu.SemaphoreType.DMA((2, 3, n_exp)),
         ],
         compiler_params=pltpu.CompilerParams(
-            collective_id=0, has_side_effects=True, vmem_limit_bytes=48 * 1024 * 1024
+            collective_id=0, has_side_effects=True, vmem_limit_bytes=60 * 1024 * 1024
         ),
         cost_estimate=pl.CostEstimate(
             flops=flops, bytes_accessed=10 * 1024 * 1024, transcendentals=4 * rows * hidden
         ),
     )(latent, cotangent, routes.reshape(1, tok), gates.reshape(1, tok), w_in, w_out)
-    output, grad_in, grad_out = pl.pallas_call(
-        store_kernel,
-        out_shape=shapes,
-        in_specs=[anywhere] * 3,
-        out_specs=(hbm, hbm, hbm),
-        scratch_shapes=[pltpu.SemaphoreType.DMA((3,))],
-        cost_estimate=pl.CostEstimate(flops=0, bytes_accessed=7 * 1024 * 1024, transcendentals=0),
-    )(*results)
     return output, grad_in.reshape(1, share, 2 * hidden), grad_out.reshape(1, share, hidden)
 
 

time: 172 us -> 69.4 us (0.40)
  Pallas kernels: 162 us -> 62.7 us
  local copies, waits for them, and re-layouts: 7.81 us -> 5.87 us
    pallas_call x1 -> x0, Pallas kernels: 104 us -> none  [fused(): pl.pallas_call(store_kernel, out_shape=shapes, in_specs=[anywhere] * 3, o...]
    pallas_call x1, Pallas kernels: 57.3 us -> 62.7 us  [fused(): pl.pallas_call(functools.partial(fused_kernel, n_exp, cap), out_shape=sha...]
    unnamed x16 -> x5, local copies, waits for them, and re-layouts: 7.81 us -> 5.87 us
where the time goes in v3:
time: 69.4 us; the launch traced here: 69.2 us
  Pallas kernels  62.7 us (90%)
  local copies, waits for them, and re-layouts  5.87 us (8%)
    pallas_call x1, Pallas kernels, fused(): pl.pallas_call(functools.partial(fused_kernel, n_exp, cap), out_shape=sha...  62.7 us
    unnamed x5, local copies, waits for them, and re-layouts  5.87 us

profile of v3, /device:TPU:9, one launch (start us, length us, event | category | flops | bytes accessed | tf_op | source)
XLA Modules:
  0.0 69.2 jit_solution(9217410430056265696)
XLA Ops:
  0.6 62.7 %shard_map.85 = (bf16[128,1024]{1,0:T(8,128)(2,1)}, f32[256,2048]{1,0:T(8,128)}, f32[256,1024]{1,0:T(8,128)}) custom-call(bf16[128,1024]{1,0:T(8,128)(2,1)} %lat_hbm.1, bf16[128,1024]{1,0:T(8,128)(2,1)} %cot_hbm.1, s32[1,128]{1,0:T(1,128)} %bitcast.6, f32[1,128]{1,0:T(1,128)} %bitcast.7, bf16[1,1024,2048]{2,1,0:T(8,128)(2,1)} %win_hbm.1, ...), custom_call_target="tpu_custom_call" | custom-call | flops 8589934592 | bytes 10485760 | tf_op jit(solution)/shard_map/pallas_call | solution.py:280
  63.3 1.7 %copy.12 = bf16[128,1024]{1,0:T(8,128)(2,1)} copy(bf16[128,1024]{1,0:T(8,128)(2,1)} %get-tuple-element.12) | data formatting | bytes 524288
  65.0 0.0 copy-start
  65.0 3.2 %copy.13 = f32[1,256,2048]{2,1,0:T(8,128)} copy(f32[1,256,2048]{2,1,0:T(8,128)} %bitcast.4) | data formatting | bytes 4194304
  68.2 0.0 copy-done
  68.2 1.0 %copy.14 = f32[1,256,1024]{2,1,0:T(8,128)} copy(f32[1,256,1024]{2,1,0:T(8,128)S(1)} %bitcast.5) | data formatting | bytes 2097152
Async XLA Ops:
  65.0 3.2 %copy-start = (f32[256,1024]{1,0:T(8,128)S(1)}, f32[256,1024]{1,0:T(8,128)}, u32[]{:S(2)}) copy-start(f32[256,1024]{1,0:T(8,128)} %get-tuple-element.8) | copy-start | bytes 3145732

commit v4 on v3

--- a/solution.py
+++ b/solution.py
@@ -28,18 +28,21 @@
     hidden = hid.shape[2]
     share = gin.shape[0]
     half = n_exp // 2
-    order = sorted(range(n_exp), key=lambda j: (min(j, n_exp - j), j))
-    far_first = list(range(1, n_exp))[::-1]
-
-    def ahead(i):
-        return (p, lax.rem(q + order[i], n_exp))
-
-    def behind(i):
-        return (p, lax.rem(q + n_exp - order[i], n_exp))
+    z, core = lax.div(q, 2), lax.rem(q, 2)
+
+    def partner_of(i):
+        line = (z, z + 1 - 2 * lax.rem(z, 2), lax.rem(z + 2, 4), 3 - z)[i // 2]
+        return line * 2 + (core if i % 2 == 0 else 1 - core)
+
+    partners = [partner_of(i) for i in range(n_exp)]
+    far_first = [4, 5, 6, 7, 2, 3, 1]
+
+    def peer(i):
+        return (p, partners[i])
 
     barrier = pltpu.get_barrier_semaphore()
     for i in range(1, n_exp):
-        pl.semaphore_signal(barrier, inc=1, device_id=ahead(i), device_id_type=MESH)
+        pl.semaphore_signal(barrier, inc=1, device_id=peer(i), device_id_type=MESH)
     pl.semaphore_signal(barrier, inc=1, device_id=xn, device_id_type=MESH)
     pl.semaphore_signal(barrier, inc=1, device_id=yn, device_id_type=MESH)
     loads = [
@@ -51,10 +54,10 @@
     for c in loads:
         c.start()
 
-    rel = lax.rem(routes_ref[...] - q + n_exp, n_exp)
-    index = jnp.zeros_like(rel)
-    for i, j in enumerate(order):
-        index = jnp.where(rel == j, i, index)
+    routes = routes_ref[...]
+    index = jnp.zeros_like(routes)
+    for i in range(1, n_exp):
+        index = jnp.where(routes == partners[i], i, index)
     i0 = lax.broadcasted_iota(jnp.int32, (tok, tok), 0)
     i1 = lax.broadcasted_iota(jnp.int32, (tok, tok), 1)
     onehot = jnp.where(i0 == index, 1.0, 0.0)
@@ -101,8 +104,8 @@
     loads[0].wait()
     place_rows(lat[...], sx, xall)
     pl.semaphore_wait(barrier, n_exp + 1)
-    for i in far_first:
-        z_copy(0, sx, at(xall, 0, i), i, ahead(i))
+    for i in (1, 4, 2, 5, 3, 6, 7):
+        z_copy(0, sx, at(xall, 0, i), i, peer(i))
 
     def g_copy(kind, src, dst, i, to):
         c = pltpu.make_async_remote_copy(
@@ -210,8 +213,7 @@
     place_rows((gates * cot[...].astype(jnp.float32)).astype(jnp.bfloat16), sdy, dyall)
     for i in range(1, n_exp):
         spread(0, i)
-        k = ([1] + far_first[:-1])[i - 1]
-        z_copy(1, sdy, at(dyall, 0, k), k, ahead(k))
+        z_copy(1, sdy, at(dyall, 0, i), i, peer(i))
     spread(1, 0)
     spread(1, 1)
     loads[2].wait()
@@ -219,7 +221,7 @@
     forward(0)
     expert_out()
     for i in far_first:
-        z_copy(2, ybuf, back.at[slots(i)], i, behind(i))
+        z_copy(2, ybuf, back.at[slots(i)], i, peer(i))
     for i in range(n_exp):
         relay(0, i)
     spread(1, 2)

time: 69.4 us -> 60.4 us (0.87); the launches traced: 69.2 us -> 59.2 us
  Pallas kernels: 62.7 us -> 52.7 us
    pallas_call x1, Pallas kernels: 62.7 us -> 52.7 us  [fused(): pl.pallas_call(functools.partial(fused_kernel, n_exp, cap), out_shape=sha...]
where the time goes in v4:
time: 60.4 us; the launch traced here: 59.2 us
  Pallas kernels  52.7 us (87%)
  local copies, waits for them, and re-layouts  5.87 us (10%)
  between operations  0.64 us (1%)
    pallas_call x1, Pallas kernels, fused(): pl.pallas_call(functools.partial(fused_kernel, n_exp, cap), out_shape=sha...  52.7 us
    unnamed x5, local copies, waits for them, and re-layouts  5.87 us

profile of v4, /device:TPU:9, one launch (start us, length us, event | category | flops | bytes accessed | tf_op | source)
XLA Modules:
  0.0 59.2 jit_solution(6862151750838354277)
XLA Ops:
  0.6 52.7 %shard_map.85 = (bf16[128,1024]{1,0:T(8,128)(2,1)}, f32[256,2048]{1,0:T(8,128)}, f32[256,1024]{1,0:T(8,128)}) custom-call(bf16[128,1024]{1,0:T(8,128)(2,1)} %lat_hbm.1, bf16[128,1024]{1,0:T(8,128)(2,1)} %cot_hbm.1, s32[1,128]{1,0:T(1,128)} %bitcast.6, f32[1,128]{1,0:T(1,128)} %bitcast.7, bf16[1,1024,2048]{2,1,0:T(8,128)(2,1)} %win_hbm.1, ...), custom_call_target="tpu_custom_call" | custom-call | flops 8589934592 | bytes 10485760 | tf_op jit(solution)/shard_map/pallas_call | solution.py:282
  53.3 1.7 %copy.12 = bf16[128,1024]{1,0:T(8,128)(2,1)} copy(bf16[128,1024]{1,0:T(8,128)(2,1)} %get-tuple-element.12) | data formatting | bytes 524288
  55.0 0.0 copy-start
  55.0 3.2 %copy.13 = f32[1,256,2048]{2,1,0:T(8,128)} copy(f32[1,256,2048]{2,1,0:T(8,128)} %bitcast.4) | data formatting | bytes 4194304
  58.2 0.0 copy-done
  58.2 1.0 %copy.14 = f32[1,256,1024]{2,1,0:T(8,128)} copy(f32[1,256,1024]{2,1,0:T(8,128)S(1)} %bitcast.5) | data formatting | bytes 2097152
Async XLA Ops:
  55.0 3.2 %copy-start = (f32[256,1024]{1,0:T(8,128)S(1)}, f32[256,1024]{1,0:T(8,128)}, u32[]{:S(2)}) copy-start(f32[256,1024]{1,0:T(8,128)} %get-tuple-element.8) | copy-start | bytes 3145732

commit v5 on v4

--- a/solution.py
+++ b/solution.py
@@ -14,9 +14,9 @@
 def fused_kernel(
     n_exp, cap,
     lat_hbm, cot_hbm, routes_ref, gates_ref, win_hbm, wout_hbm,
-    out_hbm, gin_hbm, gout_hbm,
-    out, gin, gout, lat, cot, win, wout, sx, sdy, xall, dyall, a1, a2, hid, ybuf, back, place,
-    in_sem, out_sem, zsend, zrecv, gsend, grecv,
+    out_hbm, gin_hbm, gout_hbm, gin_last_hbm, gout_last_hbm,
+    out, gin, gout, gin_last, gout_last, xt, dyt, lat, cot, win, wout, sx, sdy, xall, dyall, a1, a2, hid, ybuf, back, place,
+    in_sem, out_sem, last_sem, zsend, zrecv, gsend, grecv,
 ):
     p = lax.axis_index("dp")
     q = lax.axis_index("expert")
@@ -78,9 +78,8 @@
         kept[0, 0:cap, :] = placed[0:cap, :]
 
     def at(buf, group, i):
-        if group in (0, 3):
-            return buf.at[group, pl.ds(i * cap, cap)]
-        return buf.at[1 + i // half, pl.ds((group - 1) * (rows // 2) + (i % half) * cap, cap)]
+        first = (group % 2) * (rows // 2) + (i % half) * cap
+        return buf.at[i // half * 2 + group // 2, pl.ds(first, cap)]
 
     def slots(i):
         return pl.ds(i * cap, cap)
@@ -141,13 +140,9 @@
             g_copy(kind, 2, 3, i, xn)
 
     def take_chunk(kind, c):
-        if c in (0, 3):
-            for i in range(n_exp):
-                take(kind, c, i)
-        else:
-            for i in range((c - 1) * half, c * half):
-                take(kind, 1, i)
-                take(kind, 2, i)
+        for i in range(c // 2 * half, (c // 2 + 1) * half):
+            take(kind, c % 2 * 2, i)
+            take(kind, c % 2 * 2 + 1, i)
 
     def forward(c):
         take_chunk(0, c)
@@ -167,6 +162,8 @@
     def backward(c):
         take_chunk(1, c)
         cols = pl.ds(pl.multiple_of(p * share, share), share)
+        xt[...] = xall[c, :, cols].T
+        dyt[...] = dyall[c, :, cols].T
 
         @pl.loop(0, hidden // TILE)
         def _(h):
@@ -176,34 +173,40 @@
             d_gate = (d_hid * a1[c, :, lo]).astype(jnp.bfloat16)
             d_upper = (d_hid * a2[c, :, lo]).astype(jnp.bfloat16)
 
-            def add(ref, where, left, right):
-                term = lax.dot_general(
-                    left, right, (((0,), (0,)), ((), ())), preferred_element_type=jnp.float32
-                )
-                ref[:, where] = term if c == 0 else ref[:, where] + term
-
-            add(gin, lo, xall[c, :, cols], d_gate)
-            add(gin, hi, xall[c, :, cols], d_upper)
-            add(gout, lo, dyall[c, :, cols], hid[c, :, lo])
+            def add(total, last, where, left, right):
+                term = jnp.dot(left[...], right, preferred_element_type=jnp.float32)
+                if c == 3:
+                    last[:, where] = term.astype(jnp.bfloat16)
+                elif c == 0:
+                    total[:, where] = term
+                else:
+                    total[:, where] += term
+
+            add(gin, gin_last, lo, xt, d_gate)
+            add(gin, gin_last, hi, xt, d_upper)
+            add(gout, gout_last, lo, dyt, hid[c, :, lo])
             if c == 3:
-                for copy in stores(h):
+                for copy in last_stores(h):
                     copy.start()
 
-    def stores(h):
+    def last_stores(h):
         lo = pl.ds(pl.multiple_of(h * TILE, TILE), TILE)
         hi = pl.ds(pl.multiple_of(hidden + h * TILE, TILE), TILE)
-        pairs = ((gin, gin_hbm, lo), (gin, gin_hbm, hi), (gout, gout_hbm, lo))
+        parts = (
+            (gin_last, gin_last_hbm, lo), (gin_last, gin_last_hbm, hi), (gout_last, gout_last_hbm, lo)
+        )
         return [
-            pltpu.make_async_copy(src.at[:, where], dst.at[:, where], out_sem.at[n, h])
-            for n, (src, dst, where) in enumerate(pairs)
+            pltpu.make_async_copy(src.at[:, where], dst.at[:, where], last_sem.at[n, h])
+            for n, (src, dst, where) in enumerate(parts)
         ]
 
     def expert_out():
         @pl.loop(0, width // TILE)
         def _(l):
             tile = pl.ds(pl.multiple_of(l * TILE, TILE), TILE)
+            own = jnp.concatenate([hid[0, 0 : rows // 2, :], hid[2, 0 : rows // 2, :]], axis=0)
             ybuf[:, tile] = lax.dot_general(
-                hid[0], wout[tile, :], (((1,), (1,)), ((), ())), preferred_element_type=jnp.float32
+                own, wout[tile, :], (((1,), (1,)), ((), ())), preferred_element_type=jnp.float32
             ).astype(jnp.bfloat16)
 
         back[0:cap, :] = ybuf[0:cap, :]
@@ -211,57 +214,72 @@
     spread(0, 0)
     loads[1].wait()
     place_rows((gates * cot[...].astype(jnp.float32)).astype(jnp.bfloat16), sdy, dyall)
-    for i in range(1, n_exp):
+    def send_dy(*which):
+        for i in which:
+            z_copy(1, sdy, at(dyall, 0, i), i, peer(i))
+
+    send_dy(1, 2, 3)
+    for i in range(1, half):
         spread(0, i)
-        z_copy(1, sdy, at(dyall, 0, i), i, peer(i))
-    spread(1, 0)
-    spread(1, 1)
+    for i in range(half):
+        spread(1, i)
+    spread(0, 4)
+    send_dy(4, 5)
+    for i in range(half):
+        relay(0, i)
     loads[2].wait()
     loads[3].wait()
     forward(0)
+    spread(0, 5)
+    send_dy(6, 7)
+    relay(1, 0)
+    relay(1, 1)
+    forward(1)
+    spread(0, 6)
+    relay(1, 2)
+    relay(1, 3)
+    backward(0)
+    spread(0, 7)
+    relay(0, 4)
+    relay(0, 5)
+    backward(1)
+    relay(0, 6)
+    relay(0, 7)
+    forward(2)
+    spread(1, 4)
+    spread(1, 5)
     expert_out()
+    spread(1, 6)
+    relay(1, 4)
+    forward(3)
+    spread(1, 7)
+    relay(1, 5)
     for i in far_first:
         z_copy(2, ybuf, back.at[slots(i)], i, peer(i))
-    for i in range(n_exp):
-        relay(0, i)
-    spread(1, 2)
-    spread(1, 3)
-    relay(1, 0)
-    forward(1)
-    spread(1, 4)
-    relay(1, 1)
-    forward(2)
-    spread(1, 5)
-    relay(1, 2)
-    relay(1, 3)
-    forward(3)
-    spread(1, 6)
-    spread(1, 7)
-    relay(1, 4)
-    relay(1, 5)
-    backward(0)
     relay(1, 6)
     relay(1, 7)
-    backward(1)
     backward(2)
+    stores = [
+        pltpu.make_async_copy(src, dst, out_sem.at[n])
+        for n, (src, dst) in enumerate(((gin, gin_hbm), (gout, gout_hbm), (out, out_hbm)))
+    ]
+    stores[0].start()
+    stores[1].start()
+    backward(3)
     for i in far_first:
         z_copies[2, i].wait_recv()
-    out[...] = (
-        gates
-        * lax.dot_general(
-            place[...], back[...], (((0,), (0,)), ((), ())), preferred_element_type=jnp.float32
-        )
-    ).astype(jnp.bfloat16)
-    out_copy = pltpu.make_async_copy(out, out_hbm, in_sem.at[4])
-    out_copy.start()
-    backward(3)
+    out[...] = lax.dot_general(
+        place[...], back[...], (((0,), (0,)), ((), ())), preferred_element_type=jnp.float32
+    ).astype(jnp.bfloat16)
+    stores[2].start()
     for c in z_copies.values():
         c.wait_send()
     for c in g_copies.values():
         c.wait_send()
-    out_copy.wait()
+    for c in stores:
+        c.wait()
     for h in range(hidden // TILE):
-        for c in stores(h):
+        for c in last_stores(h):
             c.wait()
 
 
@@ -278,16 +296,22 @@
         jax.ShapeDtypeStruct((tok, width), bf16),
         jax.ShapeDtypeStruct((share, 2 * hidden), f32),
         jax.ShapeDtypeStruct((share, hidden), f32),
-    )
-    output, grad_in, grad_out = pl.pallas_call(
+        jax.ShapeDtypeStruct((share, 2 * hidden), bf16),
+        jax.ShapeDtypeStruct((share, hidden), bf16),
+    )
+    y_rows, grad_in, grad_out, last_in, last_out = pl.pallas_call(
         functools.partial(fused_kernel, n_exp, cap),
         out_shape=shapes,
         in_specs=[hbm, hbm, vmem, vmem, hbm, hbm],
-        out_specs=(hbm, hbm, hbm),
+        out_specs=(hbm,) * 5,
         scratch_shapes=[
             pltpu.VMEM((tok, width), bf16),
             pltpu.VMEM((share, 2 * hidden), f32),
             pltpu.VMEM((share, hidden), f32),
+            pltpu.VMEM((share, 2 * hidden), bf16),
+            pltpu.VMEM((share, hidden), bf16),
+            pltpu.VMEM((share, rows), bf16),
+            pltpu.VMEM((share, rows), bf16),
             pltpu.VMEM((tok, width), bf16),
             pltpu.VMEM((tok, width), bf16),
             pltpu.VMEM((width, 2 * hidden), bf16),
@@ -302,7 +326,8 @@
             pltpu.VMEM((rows, width), bf16),
             pltpu.VMEM((rows, width), bf16),
             pltpu.VMEM((rows, tok), bf16),
-            pltpu.SemaphoreType.DMA((5,)),
+            pltpu.SemaphoreType.DMA((4,)),
+            pltpu.SemaphoreType.DMA((3,)),
             pltpu.SemaphoreType.DMA((3, hidden // TILE)),
             pltpu.SemaphoreType.DMA((3, n_exp)),
             pltpu.SemaphoreType.DMA((3, n_exp)),
@@ -316,6 +341,9 @@
             flops=flops, bytes_accessed=10 * 1024 * 1024, transcendentals=4 * rows * hidden
         ),
     )(latent, cotangent, routes.reshape(1, tok), gates.reshape(1, tok), w_in, w_out)
+    output = (gates * y_rows.astype(f32)).astype(bf16)
+    grad_in = grad_in + last_in.astype(f32)
+    grad_out = grad_out + last_out.astype(f32)
     return output, grad_in.reshape(1, share, 2 * hidden), grad_out.reshape(1, share, hidden)
 
 

time: 60.4 us -> 63.3 us (1.048)
  other arithmetic: 0 us -> 6.01 us
  local copies, waits for them, and re-layouts: 5.87 us -> 0.01 us
  Pallas kernels: 52.7 us -> 55.7 us
    unnamed x5 -> x6, local copies, waits for them, and re-layouts: 5.87 us -> 0.01 us
    reshape x0 -> x2, other arithmetic: none -> 4.1 us  [the longest x1 2.52 us: fused(): grad_out.reshape(1, share, hidden)]
    pallas_call x1, Pallas kernels: 52.7 us -> 55.7 us  [fused(): pl.pallas_call(functools.partial(fused_kernel, n_exp, cap), out_shape=sha...]
    convert_element_type x0 -> x1, other arithmetic: none -> 1.91 us  [fused(): output = (gates * y_rows.astype(f32)).astype(bf16)]
where the time goes in v5:
time: 63.3 us; the launch traced here: 62.4 us
  Pallas kernels  55.7 us (88%)
  other arithmetic  6.01 us (9%)
  between operations  0.67 us (1%)
    pallas_call x1, Pallas kernels, fused(): pl.pallas_call(functools.partial(fused_kernel, n_exp, cap), out_shape=sha...  55.7 us
    reshape x1, other arithmetic, fused(): grad_out.reshape(1, share, hidden)  2.52 us
    convert_element_type x1, other arithmetic, fused(): output = (gates * y_rows.astype(f32)).astype(bf16)  1.91 us
    reshape x1, other arithmetic, fused(): grad_in.reshape(1, share, 2 * hidden)  1.58 us

profile of v5, /device:TPU:9, one launch (start us, length us, event | category | flops | bytes accessed | tf_op | source)
XLA Modules:
  0.0 62.4 jit_solution(8523898609542648442)
XLA Ops:
  0.6 0.0 copy-start.2
  0.6 55.7 %shard_map.85 = (bf16[128,1024]{1,0:T(8,128)(2,1)}, f32[256,2048]{1,0:T(8,128)}, f32[256,1024]{1,0:T(8,128)}, bf16[256,2048]{1,0:T(8,128)(2,1)}, bf16[256,1024]{1,0:T(8,128)(2,1)}) custom-call(bf16[128,1024]{1,0:T(8,128)(2,1)} %lat_hbm.1, bf16[128,1024]{1,0:T(8,128)(2,1)} %cot_hbm.1, s32[1,128]{1,0:T(1,128)} %bitcast.9, f32[1,128]{1,0:T(1,128)} %bitcast.7, ...), custom_call_target="tpu_custom_call" | custom-call | flops 8589934592 | bytes 10485760 | tf_op jit(solution)/shard_map/pallas_call | solution.py:302
  56.4 0.0 copy-start
  56.4 0.0 copy-start.1
  56.4 0.0 copy-done.2
  56.4 1.9 %multiply_convert_fusion = bf16[128,1024]{1,0:T(8,128)(2,1)} fusion(bf16[128,1024]{1,0:T(8,128)(2,1)} %get-tuple-element.8, f32[128]{0:T(128)S(1)} %bitcast.8), kind=kLoop, calls=%fused_computation.2 | loop fusion | flops 393216 | bytes 524800 | tf_op jit(solution)/shard_map/convert_element_type | solution.py:344
  58.3 2.5 %add_bitcast_fusion.1 = f32[1,256,1024]{2,1,0:T(8,128)} fusion(f32[256,1024]{1,0:T(8,128)} %get-tuple-element.11, bf16[256,1024]{1,0:T(8,128)(2,1)} %get-tuple-element.12), kind=kLoop, calls=%fused_computation.1 | loop fusion | flops 524288 | bytes 2621440 | tf_op jit(solution)/shard_map/reshape | solution.py:347
  60.9 0.0 copy-done
  60.9 0.0 copy-done.1
  60.9 1.6 %add_bitcast_fusion = f32[1,256,2048]{2,1,0:T(8,128)} fusion(f32[256,2048]{1,0:T(8,128)S(1)} %copy-done, bf16[256,2048]{1,0:T(8,128)(2,1)S(1)} %copy-done.1), kind=kLoop, calls=%fused_computation | loop fusion | flops 1048576 | bytes 5242880 | tf_op jit(solution)/shard_map/reshape | solution.py:347
Async XLA Ops:
  0.6 55.8 %copy-start.2 = (f32[128,1]{0,1:T(1,128)S(1)}, f32[128,1]{0,1:T(1,128)}, u32[]{:S(2)}) copy-start(f32[128,1]{0,1:T(1,128)} %param.9) | copy-start | bytes 1540
  56.4 4.5 %copy-start = (f32[256,2048]{1,0:T(8,128)S(1)}, f32[256,2048]{1,0:T(8,128)}, u32[]{:S(2)}) copy-start(f32[256,2048]{1,0:T(8,128)} %get-tuple-element.9) | copy-start | bytes 6291460
  56.4 4.5 %copy-start.1 = (bf16[256,2048]{1,0:T(8,128)(2,1)S(1)}, bf16[256,2048]{1,0:T(8,128)(2,1)}, u32[]{:S(2)}) copy-start(bf16[256,2048]{1,0:T(8,128)(2,1)} %get-tuple-element.10) | copy-start | bytes 3145732

commit v6 on v4

--- a/solution.py
+++ b/solution.py
@@ -15,7 +15,7 @@
     n_exp, cap,
     lat_hbm, cot_hbm, routes_ref, gates_ref, win_hbm, wout_hbm,
     out_hbm, gin_hbm, gout_hbm,
-    out, gin, gout, lat, cot, win, wout, sx, sdy, xall, dyall, a1, a2, hid, ybuf, back, place,
+    out, gin, gout, xt, dyt, lat, cot, win, wout, sx, sdy, xall, dyall, a1, a2, hid, ybuf, back, place,
     in_sem, out_sem, zsend, zrecv, gsend, grecv,
 ):
     p = lax.axis_index("dp")
@@ -167,6 +167,8 @@
     def backward(c):
         take_chunk(1, c)
         cols = pl.ds(pl.multiple_of(p * share, share), share)
+        xt[...] = xall[c, :, cols].T
+        dyt[...] = dyall[c, :, cols].T
 
         @pl.loop(0, hidden // TILE)
         def _(h):
@@ -177,14 +179,12 @@
             d_upper = (d_hid * a2[c, :, lo]).astype(jnp.bfloat16)
 
             def add(ref, where, left, right):
-                term = lax.dot_general(
-                    left, right, (((0,), (0,)), ((), ())), preferred_element_type=jnp.float32
-                )
-                ref[:, where] = term if c == 0 else ref[:, where] + term
-
-            add(gin, lo, xall[c, :, cols], d_gate)
-            add(gin, hi, xall[c, :, cols], d_upper)
-            add(gout, lo, dyall[c, :, cols], hid[c, :, lo])
+                term = jnp.dot(left[...], right, preferred_element_type=jnp.float32)
+                ref[:, where] = term if c == 1 else ref[:, where] + term
+
+            add(gin, lo, xt, d_gate)
+            add(gin, hi, xt, d_upper)
+            add(gout, lo, dyt, hid[c, :, lo])
             if c == 3:
                 for copy in stores(h):
                     copy.start()
@@ -211,39 +211,54 @@
     spread(0, 0)
     loads[1].wait()
     place_rows((gates * cot[...].astype(jnp.float32)).astype(jnp.bfloat16), sdy, dyall)
-    for i in range(1, n_exp):
-        spread(0, i)
-        z_copy(1, sdy, at(dyall, 0, i), i, peer(i))
+    def send_dy(*which):
+        for i in which:
+            z_copy(1, sdy, at(dyall, 0, i), i, peer(i))
+
+    def relays(kind, *which):
+        for i in which:
+            relay(kind, i)
+
+    send_dy(1, 2, 3)
+    spread(0, 1)
+    spread(0, 2)
+    spread(0, 3)
     spread(1, 0)
     spread(1, 1)
+    spread(0, 4)
+    send_dy(4, 5)
+    relays(0, 0, 1)
+    spread(0, 5)
+    send_dy(6, 7)
+    spread(1, 2)
+    spread(1, 3)
+    relays(0, 2, 3)
+    spread(0, 6)
+    spread(0, 7)
     loads[2].wait()
     loads[3].wait()
     forward(0)
     expert_out()
+    relays(0, 4, 5)
     for i in far_first:
         z_copy(2, ybuf, back.at[slots(i)], i, peer(i))
-    for i in range(n_exp):
-        relay(0, i)
-    spread(1, 2)
-    spread(1, 3)
-    relay(1, 0)
+    relays(1, 0, 1)
+    spread(1, 4)
+    relays(0, 6, 7)
     forward(1)
-    spread(1, 4)
-    relay(1, 1)
+    spread(1, 5)
+    relays(1, 2, 3)
     forward(2)
-    spread(1, 5)
-    relay(1, 2)
-    relay(1, 3)
+    spread(1, 6)
+    relay(1, 4)
     forward(3)
-    spread(1, 6)
     spread(1, 7)
-    relay(1, 4)
     relay(1, 5)
+    backward(1)
+    relays(1, 6, 7)
     backward(0)
-    relay(1, 6)
-    relay(1, 7)
-    backward(1)
     backward(2)
+    backward(3)
     for i in far_first:
         z_copies[2, i].wait_recv()
     out[...] = (
@@ -254,7 +269,6 @@
     ).astype(jnp.bfloat16)
     out_copy = pltpu.make_async_copy(out, out_hbm, in_sem.at[4])
     out_copy.start()
-    backward(3)
     for c in z_copies.values():
         c.wait_send()
     for c in g_copies.values():
@@ -288,6 +302,8 @@
             pltpu.VMEM((tok, width), bf16),
             pltpu.VMEM((share, 2 * hidden), f32),
             pltpu.VMEM((share, hidden), f32),
+            pltpu.VMEM((share, rows), bf16),
+            pltpu.VMEM((share, rows), bf16),
             pltpu.VMEM((tok, width), bf16),
             pltpu.VMEM((tok, width), bf16),
             pltpu.VMEM((width, 2 * hidden), bf16),
@@ -310,7 +326,7 @@
             pltpu.SemaphoreType.DMA((2, 3, n_exp)),
         ],
         compiler_params=pltpu.CompilerParams(
-            collective_id=0, has_side_effects=True, vmem_limit_bytes=60 * 1024 * 1024
+            collective_id=0, has_side_effects=True, vmem_limit_bytes=56 * 1024 * 1024
         ),
         cost_estimate=pl.CostEstimate(
             flops=flops, bytes_accessed=10 * 1024 * 1024, transcendentals=4 * rows * hidden

time: 60.4 us -> 62.4 us (1.033)
  the two profiles are of different devices: /device:TPU:9 before, /device:TPU:0 now
where the time goes in v6:
time: 62.4 us; the launch traced here: 62.3 us
  Pallas kernels  55.8 us (89%)
  local copies, waits for them, and re-layouts  5.87 us (9%)
  between operations  0.64 us (1%)
    pallas_call x1, Pallas kernels, fused(): pl.pallas_call(functools.partial(fused_kernel, n_exp, cap), out_shape=sha...  55.8 us
    unnamed x5, local copies, waits for them, and re-layouts  5.87 us

profile of v6, /device:TPU:0, one launch (start us, length us, event | category | flops | bytes accessed | tf_op | source)
XLA Modules:
  0.0 62.3 jit_solution(8925366892962791554)
XLA Ops:
  0.6 55.8 %shard_map.85 = (bf16[128,1024]{1,0:T(8,128)(2,1)}, f32[256,2048]{1,0:T(8,128)}, f32[256,1024]{1,0:T(8,128)}) custom-call(bf16[128,1024]{1,0:T(8,128)(2,1)} %lat_hbm.1, bf16[128,1024]{1,0:T(8,128)(2,1)} %cot_hbm.1, s32[1,128]{1,0:T(1,128)} %bitcast.6, f32[1,128]{1,0:T(1,128)} %bitcast.7, bf16[1,1024,2048]{2,1,0:T(8,128)(2,1)} %win_hbm.1, ...), custom_call_target="tpu_custom_call" | custom-call | flops 8589934592 | bytes 10485760 | tf_op jit(solution)/shard_map/pallas_call | solution.py:296
  56.4 1.7 %copy.12 = bf16[128,1024]{1,0:T(8,128)(2,1)} copy(bf16[128,1024]{1,0:T(8,128)(2,1)} %get-tuple-element.12) | data formatting | bytes 524288
  58.1 0.0 copy-start
  58.1 3.2 %copy.13 = f32[1,256,2048]{2,1,0:T(8,128)} copy(f32[1,256,2048]{2,1,0:T(8,128)} %bitcast.4) | data formatting | bytes 4194304
  61.3 0.0 copy-done
  61.3 1.0 %copy.14 = f32[1,256,1024]{2,1,0:T(8,128)} copy(f32[1,256,1024]{2,1,0:T(8,128)S(1)} %bitcast.5) | data formatting | bytes 2097152
Async XLA Ops:
  58.1 3.2 %copy-start = (f32[256,1024]{1,0:T(8,128)S(1)}, f32[256,1024]{1,0:T(8,128)}, u32[]{:S(2)}) copy-start(f32[256,1024]{1,0:T(8,128)} %get-tuple-element.8) | copy-start | bytes 3145732

commit v7 on v6

--- a/solution.py
+++ b/solution.py
@@ -25,7 +25,7 @@
     yn = ((1 - py) * 2 + px, q)
     tok, width = lat.shape
     rows = n_exp * cap
-    hidden = hid.shape[2]
+    hidden = hid.shape[1]
     share = gin.shape[0]
     half = n_exp // 2
     z, core = lax.div(q, 2), lax.rem(q, 2)
@@ -75,12 +75,15 @@
     def place_rows(value, sent, kept):
         placed = jnp.dot(place[...], value, preferred_element_type=jnp.float32).astype(jnp.bfloat16)
         sent[...] = placed
-        kept[0, 0:cap, :] = placed[0:cap, :]
+        kept[0:cap, :] = placed[0:cap, :]
+
+    spans = (pl.ds(0, rows), pl.ds(rows, rows * 3 // 2), pl.ds(rows * 5 // 2, rows * 3 // 2))
 
     def at(buf, group, i):
-        if group in (0, 3):
-            return buf.at[group, pl.ds(i * cap, cap)]
-        return buf.at[1 + i // half, pl.ds((group - 1) * (rows // 2) + (i % half) * cap, cap)]
+        if group == 0:
+            return buf.at[pl.ds(i * cap, cap)]
+        first = rows + (i // half) * (rows * 3 // 2) + (group - 1) * (rows // 2) + (i % half) * cap
+        return buf.at[pl.ds(first, cap)]
 
     def slots(i):
         return pl.ds(i * cap, cap)
@@ -141,51 +144,50 @@
             g_copy(kind, 2, 3, i, xn)
 
     def take_chunk(kind, c):
-        if c in (0, 3):
-            for i in range(n_exp):
-                take(kind, c, i)
-        else:
-            for i in range((c - 1) * half, c * half):
-                take(kind, 1, i)
-                take(kind, 2, i)
+        for i in range(n_exp) if c == 0 else range((c - 1) * half, c * half):
+            for group in (0,) if c == 0 else (1, 2, 3):
+                take(kind, group, i)
 
     def forward(c):
         take_chunk(0, c)
+        span = spans[c]
 
         @pl.loop(0, hidden // TILE)
         def _(h):
             lo = pl.ds(pl.multiple_of(h * TILE, TILE), TILE)
             hi = pl.ds(pl.multiple_of(hidden + h * TILE, TILE), TILE)
-            gate = jnp.dot(xall[c], win[:, lo], preferred_element_type=jnp.float32)
-            upper = jnp.dot(xall[c], win[:, hi], preferred_element_type=jnp.float32)
+            gate = jnp.dot(xall[span, :], win[:, lo], preferred_element_type=jnp.float32)
+            upper = jnp.dot(xall[span, :], win[:, hi], preferred_element_type=jnp.float32)
             sig = jax.nn.sigmoid(gate)
             swish = gate * sig
-            hid[c, :, lo] = (swish * upper).astype(jnp.bfloat16)
-            a1[c, :, lo] = upper * sig * (1.0 + gate * (1.0 - sig))
-            a2[c, :, lo] = swish
+            hid[span, lo] = (swish * upper).astype(jnp.bfloat16)
+            a1[span, lo] = upper * sig * (1.0 + gate * (1.0 - sig))
+            a2[span, lo] = swish
 
     def backward(c):
         take_chunk(1, c)
+        span = spans[c]
+        count = span.size
         cols = pl.ds(pl.multiple_of(p * share, share), share)
-        xt[...] = xall[c, :, cols].T
-        dyt[...] = dyall[c, :, cols].T
+        xt[:, 0:count] = xall[span, cols].T
+        dyt[:, 0:count] = dyall[span, cols].T
 
         @pl.loop(0, hidden // TILE)
         def _(h):
             lo = pl.ds(pl.multiple_of(h * TILE, TILE), TILE)
             hi = pl.ds(pl.multiple_of(hidden + h * TILE, TILE), TILE)
-            d_hid = jnp.dot(dyall[c], wout[:, lo], preferred_element_type=jnp.float32)
-            d_gate = (d_hid * a1[c, :, lo]).astype(jnp.bfloat16)
-            d_upper = (d_hid * a2[c, :, lo]).astype(jnp.bfloat16)
+            d_hid = jnp.dot(dyall[span, :], wout[:, lo], preferred_element_type=jnp.float32)
+            d_gate = (d_hid * a1[span, lo]).astype(jnp.bfloat16)
+            d_upper = (d_hid * a2[span, lo]).astype(jnp.bfloat16)
 
             def add(ref, where, left, right):
-                term = jnp.dot(left[...], right, preferred_element_type=jnp.float32)
-                ref[:, where] = term if c == 1 else ref[:, where] + term
+                term = jnp.dot(left[:, 0:count], right, preferred_element_type=jnp.float32)
+                ref[:, where] = term if c == 0 else ref[:, where] + term
 
             add(gin, lo, xt, d_gate)
             add(gin, hi, xt, d_upper)
-            add(gout, lo, dyt, hid[c, :, lo])
-            if c == 3:
+            add(gout, lo, dyt, hid[span, lo])
+            if c == 2:
                 for copy in stores(h):
                     copy.start()
 
@@ -203,7 +205,7 @@
         def _(l):
             tile = pl.ds(pl.multiple_of(l * TILE, TILE), TILE)
             ybuf[:, tile] = lax.dot_general(
-                hid[0], wout[tile, :], (((1,), (1,)), ((), ())), preferred_element_type=jnp.float32
+                hid[spans[0], :], wout[tile, :], (((1,), (1,)), ((), ())), preferred_element_type=jnp.float32
             ).astype(jnp.bfloat16)
 
         back[0:cap, :] = ybuf[0:cap, :]
@@ -251,14 +253,12 @@
     forward(2)
     spread(1, 6)
     relay(1, 4)
-    forward(3)
     spread(1, 7)
     relay(1, 5)
+    backward(0)
+    relays(1, 6, 7)
     backward(1)
-    relays(1, 6, 7)
-    backward(0)
     backward(2)
-    backward(3)
     for i in far_first:
         z_copies[2, i].wait_recv()
     out[...] = (
@@ -302,19 +302,19 @@
             pltpu.VMEM((tok, width), bf16),
             pltpu.VMEM((share, 2 * hidden), f32),
             pltpu.VMEM((share, hidden), f32),
-            pltpu.VMEM((share, rows), bf16),
-            pltpu.VMEM((share, rows), bf16),
+            pltpu.VMEM((share, rows * 3 // 2), bf16),
+            pltpu.VMEM((share, rows * 3 // 2), bf16),
             pltpu.VMEM((tok, width), bf16),
             pltpu.VMEM((tok, width), bf16),
             pltpu.VMEM((width, 2 * hidden), bf16),
             pltpu.VMEM((width, hidden), bf16),
             pltpu.VMEM((rows, width), bf16),
             pltpu.VMEM((rows, width), bf16),
-            pltpu.VMEM((4, rows, width), bf16),
-            pltpu.VMEM((4, rows, width), bf16),
-            pltpu.VMEM((4, rows, hidden), f32),
-            pltpu.VMEM((4, rows, hidden), f32),
-            pltpu.VMEM((4, rows, hidden), bf16),
+            pltpu.VMEM((4 * rows, width), bf16),
+            pltpu.VMEM((4 * rows, width), bf16),
+            pltpu.VMEM((4 * rows, hidden), f32),
+            pltpu.VMEM((4 * rows, hidden), f32),
+            pltpu.VMEM((4 * rows, hidden), bf16),
             pltpu.VMEM((rows, width), bf16),
             pltpu.VMEM((rows, width), bf16),
             pltpu.VMEM((rows, tok), bf16),
@@ -326,7 +326,7 @@
             pltpu.SemaphoreType.DMA((2, 3, n_exp)),
         ],
         compiler_params=pltpu.CompilerParams(
-            collective_id=0, has_side_effects=True, vmem_limit_bytes=56 * 1024 * 1024
+            collective_id=0, has_side_effects=True, vmem_limit_bytes=60 * 1024 * 1024
         ),
         cost_estimate=pl.CostEstimate(
             flops=flops, bytes_accessed=10 * 1024 * 1024, transcendentals=4 * rows * hidden

time: 62.4 us -> 62.9 us (level)
  the two profiles are of different devices: /device:TPU:0 before, /device:TPU:9 now
where the time goes in v7:
time: 62.9 us; the launch traced here: 62.6 us
  Pallas kernels  56.1 us (89%)
  local copies, waits for them, and re-layouts  5.87 us (9%)
  between operations  0.64 us (1%)
    pallas_call x1, Pallas kernels, fused(): pl.pallas_call(functools.partial(fused_kernel, n_exp, cap), out_shape=sha...  56.1 us
    unnamed x5, local copies, waits for them, and re-layouts  5.87 us

profile of v7, /device:TPU:9, one launch (start us, length us, event | category | flops | bytes accessed | tf_op | source)
XLA Modules:
  0.0 62.6 jit_solution(2483344678227080906)
XLA Ops:
  0.6 56.1 %shard_map.85 = (bf16[128,1024]{1,0:T(8,128)(2,1)}, f32[256,2048]{1,0:T(8,128)}, f32[256,1024]{1,0:T(8,128)}) custom-call(bf16[128,1024]{1,0:T(8,128)(2,1)} %lat_hbm.1, bf16[128,1024]{1,0:T(8,128)(2,1)} %cot_hbm.1, s32[1,128]{1,0:T(1,128)} %bitcast.6, f32[1,128]{1,0:T(1,128)} %bitcast.7, bf16[1,1024,2048]{2,1,0:T(8,128)(2,1)} %win_hbm.1, ...), custom_call_target="tpu_custom_call" | custom-call | flops 8589934592 | bytes 10485760 | tf_op jit(solution)/shard_map/pallas_call | solution.py:296
  56.7 1.7 %copy.12 = bf16[128,1024]{1,0:T(8,128)(2,1)} copy(bf16[128,1024]{1,0:T(8,128)(2,1)} %get-tuple-element.12) | data formatting | bytes 524288
  58.4 0.0 copy-start
  58.4 3.2 %copy.13 = f32[1,256,2048]{2,1,0:T(8,128)} copy(f32[1,256,2048]{2,1,0:T(8,128)} %bitcast.4) | data formatting | bytes 4194304
  61.6 0.0 copy-done
  61.6 1.0 %copy.14 = f32[1,256,1024]{2,1,0:T(8,128)} copy(f32[1,256,1024]{2,1,0:T(8,128)S(1)} %bitcast.5) | data formatting | bytes 2097152
Async XLA Ops:
  58.4 3.2 %copy-start = (f32[256,1024]{1,0:T(8,128)S(1)}, f32[256,1024]{1,0:T(8,128)}, u32[]{:S(2)}) copy-start(f32[256,1024]{1,0:T(8,128)} %get-tuple-element.8) | copy-start | bytes 3145732
